TPU v7x, 32 devices: a whole 2x2x4 slice. The times are simulated.
32 devices in a mesh: grp: 16 (over z, x, core), narrow: 2 (over y).
Axes of the slice: x: 2, y: 2, z: 4, core: 2. Of those that a mesh axis runs over, the one named last changes fastest.
Arguments:
- block_input: bfloat16 [2, 2048, 1024], P('narrow', 'grp'), may hold values from -6 to 6
- proj_in: bfloat16 [1024, 4096], P(('grp', 'narrow')), may hold values from -0.1875 to 0.1875
- proj_gates: bfloat16 [1024, 16], P(('grp', 'narrow')), may hold values from -0.1875 to 0.1875
- proj_out: bfloat16 [1024, 1024], P(('grp', 'narrow')), may hold values from -0.375 to 0.375
- ffn_up: bfloat16 [1024, 5632], P(('grp', 'narrow')), may hold values from -0.1875 to 0.1875
- ffn_down: bfloat16 [2816, 1024], P(('grp', 'narrow')), may hold values from -0.109375 to 0.109375
- conv_taps: float32 [4, 3072], replicated, may hold values from -3 to 3
- attn_norm: float32 [1024], replicated, may hold values from 0.5 to 1.5
- out_norm: float32 [1024], replicated, may hold values from 0.5 to 1.5
- ffn_norm: float32 [1024], replicated, may hold values from 0.5 to 1.5
- decay_log: float32 [8], replicated, may hold values from -9.91 to -2.48
- doc_lengths: int32 [2, 3], P('narrow'), may hold values from 1 to 2046, as said below
- cotangent: bfloat16 [2, 2048, 1024], P('narrow', 'grp'), may hold values from -6 to 6
Outputs:
- block_output: bfloat16 [2, 2048, 1024], P('narrow', 'grp')
- input_grad: float32 [2, 2048, 1024], P('narrow', 'grp')
- grad_proj_in: float32 [1024, 4096], P(('grp', 'narrow'))
- grad_proj_gates: float32 [1024, 16], P(('grp', 'narrow'))
- grad_proj_out: float32 [1024, 1024], P(('grp', 'narrow'))
- grad_ffn_up: float32 [1024, 5632], P(('grp', 'narrow'))
- grad_ffn_down: float32 [2816, 1024], P(('grp', 'narrow'))
- grad_conv_taps: float32 [4, 3072], replicated
- grad_attn_norm: float32 [1024], replicated
- grad_out_norm: float32 [1024], replicated
- grad_ffn_norm: float32 [1024], replicated
- grad_decay_log: float32 [8], replicated
Inputs may be any that keep to these rules, and one draw needn't show every extreme that they name: `doc_lengths`: each row lists the lengths of the 3 documents packed in order into one stream; they sum to 2048; the first document ends within the stream's first 128 tokens and the last one begins within its last 128 tokens.
All inputs are finite; a program needn't handle non-finite values.
Results may differ from a plain program's by a relative error of at most 0.012.
Values may be sent and summed in bfloat16 or wider, within the bound.
No kernel may reach another device: no remote copies, remote signals or barrier semaphores. Data moves between devices by JAX's collectives and lax.ppermute only.
A program may use at most 256 MiB of HBM per device.

v0:
```python
import functools

import jax
import jax.numpy as jnp
from jax import lax
from jax.sharding import PartitionSpec as P

D = 1024
HEADS = 8
HEAD_DIM = 128
FF = 2816
CONV = 4
CG_STEPS = 8


EPSILON = 1e-06
CG_EPSILON = 1e-06
REGULARIZER = 16.0
PRECISE = lax.Precision.HIGHEST


def passed_along(value, axis, steps):
    count = lax.axis_size(axis)
    leading, last = (max(0, -steps), min(count, count - steps))
    return lax.ppermute(value, axis, [(source, source + steps) for source in range(leading, last)])


def rms_norm(values, norm_gain):
    return (
        values * lax.rsqrt(jnp.mean(values * values, axis=-1, keepdims=True) + EPSILON) * norm_gain
    )


def split_heads(flat_rows):
    return flat_rows.reshape(flat_rows.shape[0], HEADS, HEAD_DIM).transpose(1, 0, 2)


def join_heads(stacked):
    return stacked.transpose(1, 0, 2).reshape(stacked.shape[1], HEADS * HEAD_DIM)


def unit_heads(flat_rows):
    shaped = flat_rows.reshape(flat_rows.shape[0], HEADS, HEAD_DIM)
    scaled = shaped * lax.rsqrt(jnp.sum(shaped * shaped, axis=-1, keepdims=True) + EPSILON)
    return scaled.reshape(flat_rows.shape)


def conv_features(extended, conv_taps, place_docs):
    length = extended.shape[0] - (CONV - 1)
    own_docs = place_docs[CONV - 1 :]
    summed = jnp.zeros((length, extended.shape[1]), jnp.float32)
    for offset in range(CONV):
        first_row = CONV - 1 - offset
        window = extended[first_row : first_row + length]
        same_doc = (place_docs[first_row : first_row + length] == own_docs).astype(jnp.float32)
        summed = summed + conv_taps[offset] * window * same_doc[:, None]
    activated = jax.nn.silu(summed)
    model_width = HEADS * HEAD_DIM
    return (
        unit_heads(activated[:, :model_width]),
        unit_heads(activated[:, model_width : 2 * model_width]),
        activated[:, 2 * model_width :],
    )


def gate_values(gate_logits, decay_log):
    log_decay = -jnp.exp(decay_log)[None, :] * jax.nn.sigmoid(gate_logits[:, :HEADS])
    return (log_decay, jax.nn.sigmoid(gate_logits[:, HEADS:]))


def decay_tables(log_decay, segments, carry_flag):
    cumulative = jnp.cumsum(log_decay, axis=0).T
    length = segments.shape[0]
    position = jnp.arange(length, dtype=jnp.int32)
    visible = (segments[:, None] == segments[None, :]) & (position[None, :] <= position[:, None])
    spread = (
        jnp.exp(jnp.minimum(cumulative[:, :, None] - cumulative[:, None, :], 0.0))
        * visible.astype(jnp.float32)[None]
    )
    carried = ((segments == segments[0]) & carry_flag).astype(jnp.float32)
    entry_decay = jnp.exp(cumulative) * carried[None, :]
    last_doc = (segments == segments[length - 1]).astype(jnp.float32)
    tail_decay = jnp.exp(cumulative[:, length - 1 :] - cumulative) * last_doc[None, :]
    return (spread, entry_decay, tail_decay)


def scale_state(factor, state_in):
    return factor[None, :, None, None] * state_in


def apply_system(probe_rows, key_heads, weights, entry_decay, curvature):
    carried_part = (
        jnp.einsum("hck,hkl->hcl", probe_rows, curvature, precision=PRECISE)
        * entry_decay[:, :, None]
    )
    scores = jnp.einsum("hck,hjk->hcj", probe_rows, key_heads, precision=PRECISE) * weights
    return (
        REGULARIZER * probe_rows
        + carried_part
        + jnp.einsum("hcj,hjk->hck", scores, key_heads, precision=PRECISE)
    )


def block_out(queries, key_rows, value_rows, log_decay, in_gate, state_in, segments, carry_flag):
    spread, entry_decay, tail_decay = decay_tables(log_decay, segments, carry_flag)
    weights = spread * in_gate.T[:, None, :]
    query_heads = split_heads(queries)
    key_heads = split_heads(key_rows)
    value_heads = split_heads(value_rows)
    solution = jnp.zeros_like(query_heads)
    residual = query_heads
    direction = query_heads
    norm_now = jnp.sum(residual * residual, axis=-1, keepdims=True)
    for iteration in range(CG_STEPS):
        applied = apply_system(direction, key_heads, weights, entry_decay, state_in[0])
        step_size = norm_now / (jnp.sum(direction * applied, axis=-1, keepdims=True) + CG_EPSILON)
        solution = solution + step_size * direction
        residual = residual - step_size * applied
        if iteration + 1 < CG_STEPS:
            norm_next = jnp.sum(residual * residual, axis=-1, keepdims=True)
            direction = residual + norm_next / (norm_now + CG_EPSILON) * direction
            norm_now = norm_next
    carried_part = (
        jnp.einsum("hck,hvk->hcv", solution, state_in[1], precision=PRECISE)
        * entry_decay[:, :, None]
    )
    scores = jnp.einsum("hck,hjk->hcj", solution, key_heads, precision=PRECISE) * weights
    return join_heads(
        carried_part + jnp.einsum("hcj,hjv->hcv", scores, value_heads, precision=PRECISE)
    )


def block_summary(key_rows, value_rows, log_decay, in_gate, segments, carry_flag):
    spread, entry_decay, tail_decay = decay_tables(log_decay, segments, carry_flag)
    deposit = tail_decay * in_gate.T
    key_heads = split_heads(key_rows)
    value_heads = split_heads(value_rows)
    curvature = jnp.einsum("hc,hck,hcl->hkl", deposit, key_heads, key_heads, precision=PRECISE)
    coupling = jnp.einsum("hc,hcv,hck->hvk", deposit, value_heads, key_heads, precision=PRECISE)
    return (entry_decay[:, -1], jnp.stack([curvature, coupling]))


def out_gate(mesa_out, pre_gate, out_norm):
    per_head = mesa_out.reshape(mesa_out.shape[0], HEADS, HEAD_DIM)
    normed = per_head * lax.rsqrt(jnp.mean(per_head * per_head, axis=-1, keepdims=True) + EPSILON)
    return normed.reshape(mesa_out.shape) * out_norm * jax.nn.silu(pre_gate)


def swiglu(gate_up):
    return jax.nn.silu(gate_up[:, :FF]) * gate_up[:, FF:]


def per_device(
    block_input,
    proj_in,
    proj_gates,
    proj_out,
    ffn_up,
    ffn_down,
    conv_taps,
    attn_norm,
    out_norm,
    ffn_norm,
    decay_log,
    doc_lengths,
    cotangent,
):
    token_count = block_input.shape[1]
    hidden_in = block_input[0].astype(jnp.float32)
    doc_ends = jnp.cumsum(doc_lengths[0])
    places = (
        lax.axis_index("grp") * token_count
        - (CONV - 1)
        + jnp.arange(token_count + CONV - 1, dtype=jnp.int32)
    )
    counted = jnp.sum((places[:, None] >= doc_ends[None, :]).astype(jnp.int32), axis=1)
    place_docs = jnp.where(places >= 0, counted, -1)
    own_docs = place_docs[CONV - 1 :]
    carry_flag = place_docs[CONV - 1] == place_docs[CONV - 2]
    in_full, gates_full, out_full = (
        lax.all_gather(proj_in, ("grp", "narrow"), axis=0, tiled=True),
        lax.all_gather(proj_gates, ("grp", "narrow"), axis=0, tiled=True),
        lax.all_gather(proj_out, ("grp", "narrow"), axis=0, tiled=True),
    )
    normed, norm_one_pull = jax.vjp(rms_norm, hidden_in, attn_norm)
    normed_low = normed.astype(jnp.bfloat16)
    projected = jnp.dot(normed_low, in_full, preferred_element_type=jnp.float32)
    gate_logits = jnp.dot(normed_low, gates_full, preferred_element_type=jnp.float32)
    features = projected[:, : 3 * D]
    pre_gate = projected[:, 3 * D :]
    before_rows = passed_along(features[token_count - (CONV - 1) :], "grp", 1)
    extended = jnp.concatenate([before_rows, features], axis=0)
    (queries, key_rows, value_rows), conv_pull = jax.vjp(
        functools.partial(conv_features, place_docs=place_docs), extended, conv_taps
    )
    (log_decay, in_gate), gate_pull = jax.vjp(gate_values, gate_logits, decay_log)
    summary_fn = functools.partial(block_summary, segments=own_docs, carry_flag=carry_flag)
    (through, fresh_state), summary_pull = jax.vjp(
        summary_fn, key_rows, value_rows, log_decay, in_gate
    )

    def relay_forward(relay_turn, carried_state):
        return passed_along(scale_state(through, carried_state) + fresh_state, "grp", 1)

    incoming = lax.fori_loop(
        0, lax.axis_size("grp") - 1, relay_forward, jnp.zeros_like(fresh_state)
    )
    out_fn = functools.partial(block_out, segments=own_docs, carry_flag=carry_flag)
    mesa_out, out_pull = jax.vjp(
        out_fn, queries, key_rows, value_rows, log_decay, in_gate, incoming
    )
    gated_out, gate_out_pull = jax.vjp(out_gate, mesa_out, pre_gate, out_norm)
    gated_low = gated_out.astype(jnp.bfloat16)
    hidden = hidden_in + jnp.dot(gated_low, out_full, preferred_element_type=jnp.float32)
    up_full, down_full = (
        lax.all_gather(ffn_up, ("grp", "narrow"), axis=0, tiled=True),
        lax.all_gather(ffn_down, ("grp", "narrow"), axis=0, tiled=True),
    )
    normed_two, norm_two_pull = jax.vjp(rms_norm, hidden, ffn_norm)
    normed_two_low = normed_two.astype(jnp.bfloat16)
    gate_up = jnp.dot(normed_two_low, up_full, preferred_element_type=jnp.float32)
    activated, swiglu_pull = jax.vjp(swiglu, gate_up)
    act_low = activated.astype(jnp.bfloat16)
    block_output = hidden + jnp.dot(act_low, down_full, preferred_element_type=jnp.float32)
    up_full, down_full, in_full, gates_full, out_full = (
        lax.all_gather(ffn_up, ("grp", "narrow"), axis=0, tiled=True),
        lax.all_gather(ffn_down, ("grp", "narrow"), axis=0, tiled=True),
        lax.all_gather(proj_in, ("grp", "narrow"), axis=0, tiled=True),
        lax.all_gather(proj_gates, ("grp", "narrow"), axis=0, tiled=True),
        lax.all_gather(proj_out, ("grp", "narrow"), axis=0, tiled=True),
    )
    group_rows = (
        lax.all_gather(normed_low, "narrow", axis=0, tiled=True),
        lax.all_gather(gated_low, "narrow", axis=0, tiled=True),
        lax.all_gather(normed_two_low, "narrow", axis=0, tiled=True),
        lax.all_gather(act_low, "narrow", axis=0, tiled=True),
    )
    grad_output = cotangent[0]
    grad_act = jnp.dot(grad_output, down_full.T, preferred_element_type=jnp.float32)
    (grad_gate_up,) = swiglu_pull(grad_act)
    grad_gate_low = grad_gate_up.astype(jnp.bfloat16)
    grad_normed_two = jnp.dot(grad_gate_low, up_full.T, preferred_element_type=jnp.float32)
    grad_hidden_norm, grad_ffn_norm = norm_two_pull(grad_normed_two)
    grad_hidden = grad_output.astype(jnp.float32) + grad_hidden_norm
    grad_branch = grad_hidden.astype(jnp.bfloat16)
    grad_gated = jnp.dot(grad_branch, out_full.T, preferred_element_type=jnp.float32)
    grad_mesa, grad_pre_gate, grad_out_norm = gate_out_pull(grad_gated)
    grad_queries, grad_keys_out, grad_values_out, grad_decay_out, grad_gate_out, grad_incoming = (
        out_pull(grad_mesa)
    )

    def relay_backward(relay_turn, later_grad):
        return passed_along(grad_incoming + scale_state(through, later_grad), "grp", -1)

    after_grad = lax.fori_loop(
        0, lax.axis_size("grp") - 1, relay_backward, jnp.zeros_like(grad_incoming)
    )
    grad_through = jnp.sum(after_grad * incoming, axis=(0, 2, 3))
    grad_keys_sum, grad_values_sum, grad_decay_sum, grad_gate_sum = summary_pull(
        (grad_through, after_grad)
    )
    grad_logits, grad_decay_log = gate_pull(
        (grad_decay_out + grad_decay_sum, grad_gate_out + grad_gate_sum)
    )
    grad_extended, grad_conv_taps = conv_pull(
        (grad_queries, grad_keys_out + grad_keys_sum, grad_values_out + grad_values_sum)
    )
    returned = passed_along(grad_extended[: CONV - 1], "grp", -1)
    grad_features = grad_extended[CONV - 1 :] + jnp.pad(
        returned, ((token_count - (CONV - 1), 0), (0, 0))
    )
    grad_projected = jnp.concatenate([grad_features, grad_pre_gate], axis=1).astype(jnp.bfloat16)
    grad_logits_low = grad_logits.astype(jnp.bfloat16)
    grad_normed = jnp.dot(grad_projected, in_full.T, preferred_element_type=jnp.float32) + jnp.dot(
        grad_logits_low, gates_full.T, preferred_element_type=jnp.float32
    )
    grad_input_norm, grad_attn_norm = norm_one_pull(grad_normed)
    input_grad = grad_hidden + grad_input_norm
    column_parts = (
        lax.all_to_all(grad_output, "narrow", split_axis=1, concat_axis=0, tiled=True),
        lax.all_to_all(grad_gate_low, "narrow", split_axis=1, concat_axis=0, tiled=True),
        lax.all_to_all(grad_branch, "narrow", split_axis=1, concat_axis=0, tiled=True),
        lax.all_to_all(grad_projected, "narrow", split_axis=1, concat_axis=0, tiled=True),
        lax.all_to_all(grad_logits_low, "narrow", split_axis=1, concat_axis=0, tiled=True),
    )
    group_normed, group_gated, group_normed_two, group_act = group_rows
    part_in = jnp.dot(group_normed.T, column_parts[3], preferred_element_type=jnp.float32)
    part_gates = jnp.dot(group_normed.T, column_parts[4], preferred_element_type=jnp.float32)
    part_out = jnp.dot(group_gated.T, column_parts[2], preferred_element_type=jnp.float32)
    part_up = jnp.dot(group_normed_two.T, column_parts[1], preferred_element_type=jnp.float32)
    part_down = jnp.dot(group_act.T, column_parts[0], preferred_element_type=jnp.float32)
    outer = (
        lax.psum_scatter(part_in, "grp", scatter_dimension=0, tiled=True),
        lax.psum_scatter(part_gates, "grp", scatter_dimension=0, tiled=True),
        lax.psum_scatter(part_out, "grp", scatter_dimension=0, tiled=True),
        lax.psum_scatter(part_up, "grp", scatter_dimension=0, tiled=True),
        lax.psum_scatter(part_down, "grp", scatter_dimension=0, tiled=True),
    )
    placed = (
        lax.all_to_all(outer[0], "narrow", split_axis=0, concat_axis=1, tiled=True),
        lax.all_to_all(outer[1], "narrow", split_axis=0, concat_axis=1, tiled=True),
        lax.all_to_all(outer[2], "narrow", split_axis=0, concat_axis=1, tiled=True),
        lax.all_to_all(outer[3], "narrow", split_axis=0, concat_axis=1, tiled=True),
        lax.all_to_all(outer[4], "narrow", split_axis=0, concat_axis=1, tiled=True),
    )
    small_sums = lax.psum(
        (grad_conv_taps, grad_attn_norm, grad_out_norm, grad_ffn_norm, grad_decay_log),
        ("grp", "narrow"),
    )
    return (
        block_output.astype(jnp.bfloat16)[None],
        input_grad[None],
        placed[0],
        placed[1],
        placed[2],
        placed[3],
        placed[4],
        small_sums[0],
        small_sums[1],
        small_sums[2],
        small_sums[3],
        small_sums[4],
    )


def solution(mesh):
    return jax.shard_map(
        per_device,
        mesh=mesh,
        in_specs=(
            P("narrow", "grp", None),
            P(("grp", "narrow"), None),
            P(("grp", "narrow"), None),
            P(("grp", "narrow"), None),
            P(("grp", "narrow"), None),
            P(("grp", "narrow"), None),
            P(),
            P(),
            P(),
            P(),
            P(),
            P("narrow", None),
            P("narrow", "grp", None),
        ),
        out_specs=(
            P("narrow", "grp", None),
            P("narrow", "grp", None),
            P(("grp", "narrow"), None),
            P(("grp", "narrow"), None),
            P(("grp", "narrow"), None),
            P(("grp", "narrow"), None),
            P(("grp", "narrow"), None),
            P(),
            P(),
            P(),
            P(),
            P(),
        ),
        check_vma=False,
    )
```

profile of v0, /device:TPU:0, one launch (start us, length us, event | category | flops | bytes accessed | tf_op | source)
XLA Modules:
  0.0 1476.3 jit_solution(13465730138253445303)
XLA Ops:
  17.3 71.2 %all-gather = bf16[32,32,16]{1,2,0:T(8,128)(2,1)S(1)} all-gather(bf16[1,32,16]{1,2,0:T(8,128)(2,1)S(1)} %bitcast.1180), channel_id=1, replica_groups=mesh['grp'=16,'narrow'=2] {'grp','narrow'}, dimensions={0}, use_global_device_ids=true | all-gather | bytes 33792 | tf_op jit(solution)/shard_map/all_gather | solution.py:182
  99.4 10.3 all_gather.37
  117.4 305.7 %while.20 = (s32[]{:T(128)}, f32[2,8,128,128]{3,2,1,0:T(8,128)S(1)}, f32[8,1]{0,1:T(1,128)S(1)}, f32[2,8,128,128]{3,2,1,0:T(8,128)S(1)}, s32[]{:T(128)}) while((s32[]{:T(128)}, f32[2,8,128,128]{3,2,1,0:T(8,128)S(1)}, f32[8,1]{0,1:T(1,128)S(1)}, f32[2,8,128,128]{3,2,1,0:T(8,128)S(1)}, s32[]{:T(128)}) %tuple.181), condition=%wide.region_8.9_spmd, body=%wide.region_7.8_spmd.sunk | while | flops 524290 | bytes 7340165 | solution.py:205
  124.1 12.4 collective-permute-start
  140.2 15.8 %collective-permute-start = (f32[2,8,128,128]{3,2,1,0:T(8,128)}, f32[2,8,128,128]{3,2,1,0:T(8,128)S(1)}, u32[]{:S(2)}, u32[]{:S(2)}) collective-permute-start(f32[2,8,128,128]{3,2,1,0:T(8,128)} %multiply_add_fusion.28), channel_id=1, source_target_pairs={{0,2},{2,4},{4,6},{6,8},{8,10},{10,12},{12,14},{14,16},{16,18},{18... | collective-permute-start | bytes 3145736 | tf_op jit(solution)/shard_map/while/body/eval_jaxpr/ppermute | solution.py:25
  159.6 16.5 %collective-permute-start = (f32[2,8,128,128]{3,2,1,0:T(8,128)}, f32[2,8,128,128]{3,2,1,0:T(8,128)S(1)}, u32[]{:S(2)}, u32[]{:S(2)}) collective-permute-start(f32[2,8,128,128]{3,2,1,0:T(8,128)} %multiply_add_fusion.28), channel_id=1, source_target_pairs={{0,2},{2,4},{4,6},{6,8},{8,10},{10,12},{12,14},{14,16},{16,18},{18... | collective-permute-start | bytes 3145736 | tf_op jit(solution)/shard_map/while/body/eval_jaxpr/ppermute | solution.py:25
  179.6 24.2 %collective-permute-start = (f32[2,8,128,128]{3,2,1,0:T(8,128)}, f32[2,8,128,128]{3,2,1,0:T(8,128)S(1)}, u32[]{:S(2)}, u32[]{:S(2)}) collective-permute-start(f32[2,8,128,128]{3,2,1,0:T(8,128)} %multiply_add_fusion.28), channel_id=1, source_target_pairs={{0,2},{2,4},{4,6},{6,8},{8,10},{10,12},{12,14},{14,16},{16,18},{18... | collective-permute-start | bytes 3145736 | tf_op jit(solution)/shard_map/while/body/eval_jaxpr/ppermute | solution.py:25
  207.4 16.8 %collective-permute-start = (f32[2,8,128,128]{3,2,1,0:T(8,128)}, f32[2,8,128,128]{3,2,1,0:T(8,128)S(1)}, u32[]{:S(2)}, u32[]{:S(2)}) collective-permute-start(f32[2,8,128,128]{3,2,1,0:T(8,128)} %multiply_add_fusion.28), channel_id=1, source_target_pairs={{0,2},{2,4},{4,6},{6,8},{8,10},{10,12},{12,14},{14,16},{16,18},{18... | collective-permute-start | bytes 3145736 | tf_op jit(solution)/shard_map/while/body/eval_jaxpr/ppermute | solution.py:25
  227.8 25.3 %collective-permute-start = (f32[2,8,128,128]{3,2,1,0:T(8,128)}, f32[2,8,128,128]{3,2,1,0:T(8,128)S(1)}, u32[]{:S(2)}, u32[]{:S(2)}) collective-permute-start(f32[2,8,128,128]{3,2,1,0:T(8,128)} %multiply_add_fusion.28), channel_id=1, source_target_pairs={{0,2},{2,4},{4,6},{6,8},{8,10},{10,12},{12,14},{14,16},{16,18},{18... | collective-permute-start | bytes 3145736 | tf_op jit(solution)/shard_map/while/body/eval_jaxpr/ppermute | solution.py:25
  256.7 21.5 %collective-permute-start = (f32[2,8,128,128]{3,2,1,0:T(8,128)}, f32[2,8,128,128]{3,2,1,0:T(8,128)S(1)}, u32[]{:S(2)}, u32[]{:S(2)}) collective-permute-start(f32[2,8,128,128]{3,2,1,0:T(8,128)} %multiply_add_fusion.28), channel_id=1, source_target_pairs={{0,2},{2,4},{4,6},{6,8},{8,10},{10,12},{12,14},{14,16},{16,18},{18... | collective-permute-start | bytes 3145736 | tf_op jit(solution)/shard_map/while/body/eval_jaxpr/ppermute | solution.py:25
  281.8 16.3 %collective-permute-start = (f32[2,8,128,128]{3,2,1,0:T(8,128)}, f32[2,8,128,128]{3,2,1,0:T(8,128)S(1)}, u32[]{:S(2)}, u32[]{:S(2)}) collective-permute-start(f32[2,8,128,128]{3,2,1,0:T(8,128)} %multiply_add_fusion.28), channel_id=1, source_target_pairs={{0,2},{2,4},{4,6},{6,8},{8,10},{10,12},{12,14},{14,16},{16,18},{18... | collective-permute-start | bytes 3145736 | tf_op jit(solution)/shard_map/while/body/eval_jaxpr/ppermute | solution.py:25
  301.7 17.2 %collective-permute-start = (f32[2,8,128,128]{3,2,1,0:T(8,128)}, f32[2,8,128,128]{3,2,1,0:T(8,128)S(1)}, u32[]{:S(2)}, u32[]{:S(2)}) collective-permute-start(f32[2,8,128,128]{3,2,1,0:T(8,128)} %multiply_add_fusion.28), channel_id=1, source_target_pairs={{0,2},{2,4},{4,6},{6,8},{8,10},{10,12},{12,14},{14,16},{16,18},{18... | collective-permute-start | bytes 3145736 | tf_op jit(solution)/shard_map/while/body/eval_jaxpr/ppermute | solution.py:25
  322.4 16.2 %collective-permute-start = (f32[2,8,128,128]{3,2,1,0:T(8,128)}, f32[2,8,128,128]{3,2,1,0:T(8,128)S(1)}, u32[]{:S(2)}, u32[]{:S(2)}) collective-permute-start(f32[2,8,128,128]{3,2,1,0:T(8,128)} %multiply_add_fusion.28), channel_id=1, source_target_pairs={{0,2},{2,4},{4,6},{6,8},{8,10},{10,12},{12,14},{14,16},{16,18},{18... | collective-permute-start | bytes 3145736 | tf_op jit(solution)/shard_map/while/body/eval_jaxpr/ppermute | solution.py:25
  342.2 23.1 %collective-permute-start = (f32[2,8,128,128]{3,2,1,0:T(8,128)}, f32[2,8,128,128]{3,2,1,0:T(8,128)S(1)}, u32[]{:S(2)}, u32[]{:S(2)}) collective-permute-start(f32[2,8,128,128]{3,2,1,0:T(8,128)} %multiply_add_fusion.28), channel_id=1, source_target_pairs={{0,2},{2,4},{4,6},{6,8},{8,10},{10,12},{12,14},{14,16},{16,18},{18... | collective-permute-start | bytes 3145736 | tf_op jit(solution)/shard_map/while/body/eval_jaxpr/ppermute | solution.py:25
  369.0 14.8 %collective-permute-start = (f32[2,8,128,128]{3,2,1,0:T(8,128)}, f32[2,8,128,128]{3,2,1,0:T(8,128)S(1)}, u32[]{:S(2)}, u32[]{:S(2)}) collective-permute-start(f32[2,8,128,128]{3,2,1,0:T(8,128)} %multiply_add_fusion.28), channel_id=1, source_target_pairs={{0,2},{2,4},{4,6},{6,8},{8,10},{10,12},{12,14},{14,16},{16,18},{18... | collective-permute-start | bytes 3145736 | tf_op jit(solution)/shard_map/while/body/eval_jaxpr/ppermute | solution.py:25
  387.4 14.8 %collective-permute-start = (f32[2,8,128,128]{3,2,1,0:T(8,128)}, f32[2,8,128,128]{3,2,1,0:T(8,128)S(1)}, u32[]{:S(2)}, u32[]{:S(2)}) collective-permute-start(f32[2,8,128,128]{3,2,1,0:T(8,128)} %multiply_add_fusion.28), channel_id=1, source_target_pairs={{0,2},{2,4},{4,6},{6,8},{8,10},{10,12},{12,14},{14,16},{16,18},{18... | collective-permute-start | bytes 3145736 | tf_op jit(solution)/shard_map/while/body/eval_jaxpr/ppermute | solution.py:25
  405.8 14.8 %collective-permute-start = (f32[2,8,128,128]{3,2,1,0:T(8,128)}, f32[2,8,128,128]{3,2,1,0:T(8,128)S(1)}, u32[]{:S(2)}, u32[]{:S(2)}) collective-permute-start(f32[2,8,128,128]{3,2,1,0:T(8,128)} %multiply_add_fusion.28), channel_id=1, source_target_pairs={{0,2},{2,4},{4,6},{6,8},{8,10},{10,12},{12,14},{14,16},{16,18},{18... | collective-permute-start | bytes 3145736 | tf_op jit(solution)/shard_map/while/body/eval_jaxpr/ppermute | solution.py:25
  470.5 7.1 all_gather.38
  481.8 7.7 fusion.602
  489.5 6.9 fusion.474
  582.4 302.0 %while.21 = (s32[]{:T(128)}, f32[2,8,128,128]{3,2,1,0:T(8,128)}, f32[8,1]{0,1:T(1,128)S(1)}, f32[2,8,128,128]{3,2,1,0:T(8,128)}, s32[]{:T(128)}) while((s32[]{:T(128)}, f32[2,8,128,128]{3,2,1,0:T(8,128)}, f32[8,1]{0,1:T(1,128)S(1)}, f32[2,8,128,128]{3,2,1,0:T(8,128)}, s32[]{:T(128)}) %tuple.207), condition=%wide.region_51.52_spmd, body=%wide.region_50.51_spmd.sunk | while | flops 524290 | bytes 7340165 | solution.py:255
  586.8 14.8 %collective-permute-done.1 = f32[2,8,128,128]{3,2,1,0:T(8,128)} collective-permute-done((f32[2,8,128,128]{3,2,1,0:T(8,128)}, f32[2,8,128,128]{3,2,1,0:T(8,128)}, u32[]{:S(2)}, u32[]{:S(2)}) %collective-permute-start.1) | collective-permute-done | bytes 1048608 | tf_op jit(solution)/shard_map/while/body/eval_jaxpr/ppermute | solution.py:25
  605.6 17.8 %collective-permute-done.1 = f32[2,8,128,128]{3,2,1,0:T(8,128)} collective-permute-done((f32[2,8,128,128]{3,2,1,0:T(8,128)}, f32[2,8,128,128]{3,2,1,0:T(8,128)}, u32[]{:S(2)}, u32[]{:S(2)}) %collective-permute-start.1) | collective-permute-done | bytes 1048608 | tf_op jit(solution)/shard_map/while/body/eval_jaxpr/ppermute | solution.py:25
  627.4 15.1 %collective-permute-done.1 = f32[2,8,128,128]{3,2,1,0:T(8,128)} collective-permute-done((f32[2,8,128,128]{3,2,1,0:T(8,128)}, f32[2,8,128,128]{3,2,1,0:T(8,128)}, u32[]{:S(2)}, u32[]{:S(2)}) %collective-permute-start.1) | collective-permute-done | bytes 1048608 | tf_op jit(solution)/shard_map/while/body/eval_jaxpr/ppermute | solution.py:25
  646.6 17.5 %collective-permute-done.1 = f32[2,8,128,128]{3,2,1,0:T(8,128)} collective-permute-done((f32[2,8,128,128]{3,2,1,0:T(8,128)}, f32[2,8,128,128]{3,2,1,0:T(8,128)}, u32[]{:S(2)}, u32[]{:S(2)}) %collective-permute-start.1) | collective-permute-done | bytes 1048608 | tf_op jit(solution)/shard_map/while/body/eval_jaxpr/ppermute | solution.py:25
  668.0 16.0 %collective-permute-done.1 = f32[2,8,128,128]{3,2,1,0:T(8,128)} collective-permute-done((f32[2,8,128,128]{3,2,1,0:T(8,128)}, f32[2,8,128,128]{3,2,1,0:T(8,128)}, u32[]{:S(2)}, u32[]{:S(2)}) %collective-permute-start.1) | collective-permute-done | bytes 1048608 | tf_op jit(solution)/shard_map/while/body/eval_jaxpr/ppermute | solution.py:25
  688.1 16.0 %collective-permute-done.1 = f32[2,8,128,128]{3,2,1,0:T(8,128)} collective-permute-done((f32[2,8,128,128]{3,2,1,0:T(8,128)}, f32[2,8,128,128]{3,2,1,0:T(8,128)}, u32[]{:S(2)}, u32[]{:S(2)}) %collective-permute-start.1) | collective-permute-done | bytes 1048608 | tf_op jit(solution)/shard_map/while/body/eval_jaxpr/ppermute | solution.py:25
  708.1 16.0 %collective-permute-done.1 = f32[2,8,128,128]{3,2,1,0:T(8,128)} collective-permute-done((f32[2,8,128,128]{3,2,1,0:T(8,128)}, f32[2,8,128,128]{3,2,1,0:T(8,128)}, u32[]{:S(2)}, u32[]{:S(2)}) %collective-permute-start.1) | collective-permute-done | bytes 1048608 | tf_op jit(solution)/shard_map/while/body/eval_jaxpr/ppermute | solution.py:25
  728.1 16.0 %collective-permute-done.1 = f32[2,8,128,128]{3,2,1,0:T(8,128)} collective-permute-done((f32[2,8,128,128]{3,2,1,0:T(8,128)}, f32[2,8,128,128]{3,2,1,0:T(8,128)}, u32[]{:S(2)}, u32[]{:S(2)}) %collective-permute-start.1) | collective-permute-done | bytes 1048608 | tf_op jit(solution)/shard_map/while/body/eval_jaxpr/ppermute | solution.py:25
  748.2 16.0 %collective-permute-done.1 = f32[2,8,128,128]{3,2,1,0:T(8,128)} collective-permute-done((f32[2,8,128,128]{3,2,1,0:T(8,128)}, f32[2,8,128,128]{3,2,1,0:T(8,128)}, u32[]{:S(2)}, u32[]{:S(2)}) %collective-permute-start.1) | collective-permute-done | bytes 1048608 | tf_op jit(solution)/shard_map/while/body/eval_jaxpr/ppermute | solution.py:25
  768.2 16.0 %collective-permute-done.1 = f32[2,8,128,128]{3,2,1,0:T(8,128)} collective-permute-done((f32[2,8,128,128]{3,2,1,0:T(8,128)}, f32[2,8,128,128]{3,2,1,0:T(8,128)}, u32[]{:S(2)}, u32[]{:S(2)}) %collective-permute-start.1) | collective-permute-done | bytes 1048608 | tf_op jit(solution)/shard_map/while/body/eval_jaxpr/ppermute | solution.py:25
  788.2 16.0 %collective-permute-done.1 = f32[2,8,128,128]{3,2,1,0:T(8,128)} collective-permute-done((f32[2,8,128,128]{3,2,1,0:T(8,128)}, f32[2,8,128,128]{3,2,1,0:T(8,128)}, u32[]{:S(2)}, u32[]{:S(2)}) %collective-permute-start.1) | collective-permute-done | bytes 1048608 | tf_op jit(solution)/shard_map/while/body/eval_jaxpr/ppermute | solution.py:25
  808.3 16.0 %collective-permute-done.1 = f32[2,8,128,128]{3,2,1,0:T(8,128)} collective-permute-done((f32[2,8,128,128]{3,2,1,0:T(8,128)}, f32[2,8,128,128]{3,2,1,0:T(8,128)}, u32[]{:S(2)}, u32[]{:S(2)}) %collective-permute-start.1) | collective-permute-done | bytes 1048608 | tf_op jit(solution)/shard_map/while/body/eval_jaxpr/ppermute | solution.py:25
  828.3 16.0 %collective-permute-done.1 = f32[2,8,128,128]{3,2,1,0:T(8,128)} collective-permute-done((f32[2,8,128,128]{3,2,1,0:T(8,128)}, f32[2,8,128,128]{3,2,1,0:T(8,128)}, u32[]{:S(2)}, u32[]{:S(2)}) %collective-permute-start.1) | collective-permute-done | bytes 1048608 | tf_op jit(solution)/shard_map/while/body/eval_jaxpr/ppermute | solution.py:25
  848.3 16.0 %collective-permute-done.1 = f32[2,8,128,128]{3,2,1,0:T(8,128)} collective-permute-done((f32[2,8,128,128]{3,2,1,0:T(8,128)}, f32[2,8,128,128]{3,2,1,0:T(8,128)}, u32[]{:S(2)}, u32[]{:S(2)}) %collective-permute-start.1) | collective-permute-done | bytes 1048608 | tf_op jit(solution)/shard_map/while/body/eval_jaxpr/ppermute | solution.py:25
  868.4 16.0 %collective-permute-done.1 = f32[2,8,128,128]{3,2,1,0:T(8,128)} collective-permute-done((f32[2,8,128,128]{3,2,1,0:T(8,128)}, f32[2,8,128,128]{3,2,1,0:T(8,128)}, u32[]{:S(2)}, u32[]{:S(2)}) %collective-permute-start.1) | collective-permute-done | bytes 1048608 | tf_op jit(solution)/shard_map/while/body/eval_jaxpr/ppermute | solution.py:25
  943.8 25.3 %all-gather.15.cloned.1.call-done = bf16[256,2816]{1,0:T(8,128)(2,1)} async-done(((bf16[128,2816]{1,0:T(8,128)(2,1)}), bf16[256,2816]{1,0:T(8,128)(2,1)}) %all-gather.15.cloned.1.call-update) | async-done | bytes 1441808 | tf_op jit(solution)/shard_map/all_gather | solution.py:236
  988.8 9.9 fusion.15
  1010.9 17.3 %all_to_all.187 = bf16[128,2,2048]{2,0,1:T(8,128)(2,1)S(1)} all-to-all(bf16[128,2,2048]{2,0,1:T(8,128)(2,1)S(1)} %bitcast.1140), channel_id=1, replica_groups=mesh['grp'=16,'narrow'=2] {'narrow'}, dimensions={1} | all-to-all | bytes 2097152 | tf_op jit(solution)/shard_map/all_to_all | solution.py:283
  1039.3 24.2 %all_gather.39 = bf16[256,1024]{1,0:T(8,128)(2,1)S(1)} all-gather(bf16[128,1024]{1,0:T(8,128)(2,1)S(1)} %copy-done.147), channel_id=1, replica_groups=mesh['grp'=16,'narrow'=2] {'narrow'}, dimensions={0}, use_global_device_ids=true | all-gather | bytes 786432 | tf_op jit(solution)/shard_map/all_gather | solution.py:235
  1063.4 6.0 fusion.606
  1083.7 10.1 reduce-scatter.10.cloned.1.call-done
  1101.6 76.6 %reduce-scatter.14.cloned.1.call-done = f32[176,512]{1,0:T(8,128)} async-done(((f32[2816,512]{1,0:T(8,128)}), f32[176,512]{1,0:T(8,128)}) %reduce-scatter.14.cloned.1.call-update) | async-done | bytes 360464 | tf_op jit(solution)/shard_map/reduce_scatter | solution.py:297
  1181.7 5.9 all-to-all-done.9
  1187.6 98.6 %reduce-scatter.8.cloned.1.call-done = f32[64,2048]{1,0:T(8,128)} async-done(((f32[1024,2048]{1,0:T(8,128)}), f32[64,2048]{1,0:T(8,128)}) %reduce-scatter.8.cloned.1.call-update) | async-done | bytes 524304 | tf_op jit(solution)/shard_map/reduce_scatter | solution.py:293
  1289.7 7.1 fusion.25
  1297.9 118.2 %reduce-scatter.12.cloned.1.call-done = f32[64,2816]{1,0:T(8,128)} async-done(((f32[1024,2816]{1,0:T(8,128)}), f32[64,2816]{1,0:T(8,128)}) %reduce-scatter.12.cloned.1.call-update) | async-done | bytes 720912 | tf_op jit(solution)/shard_map/reduce_scatter | solution.py:296
  1421.9 42.2 %all-reduce.27 = (f32[4,3072]{1,0:T(4,128)}, f32[1024]{0:T(1024)}, f32[1024]{0:T(1024)}, f32[1024]{0:T(1024)}, f32[8]{0:T(128)}) all-reduce(f32[4,3072]{1,0:T(4,128)S(1)} %pad_add_fusion.3, f32[1024]{0:T(1024)S(1)} %get-tuple-element.104, f32[1024]{0:T(1024)S(1)} %copy-done.297, ...), channel_id=1, replica_groups=mesh['grp'=16,'narrow'=2] {'grp','narrow'}, use_global_device_ids=true, to_apply=%region_80.81 | all-reduce | flops 15368 | bytes 122944 | tf_op jit(solution)/shard_map/psum | solution.py:306
  (995 shorter events, 419.4 us)
Async XLA Ops:
  7.2 86.1 %all-gather.7.cloned.1.call-start = ((), (), s32[]{:S(2)}) async-start(), calls=%async_computation.15 | async-start | bytes 8650752 | tf_op jit(solution)/shard_map/all_gather | solution.py:181
  8.0 469.6 %all-gather.9.cloned.1.call-start = ((), (), s32[]{:S(2)}) async-start(), calls=%async_computation.16 | async-start | bytes 2162688 | tf_op jit(solution)/shard_map/all_gather | solution.py:183
  8.7 473.1 %all-gather.11.cloned.1.call-start = ((), (), s32[]{:S(2)}) async-start(), calls=%async_computation.17 | async-start | bytes 11894784 | tf_op jit(solution)/shard_map/all_gather | solution.py:216
  11.3 98.6 %all-to-all-start.8 = ((bf16[128,2,512]{0,2,1:T(8,128)(2,1)}), bf16[128,2,512]{0,2,1:T(8,128)(2,1)S(1)}, u32[]{:S(2)}, u32[]{:S(2)}) async-start(bf16[128,2,512]{0,2,1:T(8,128)(2,1)} %bitcast.141), calls=%async_computation.11 | async-start | bytes 524288 | tf_op jit(solution)/shard_map/all_to_all | solution.py:280
  15.5 474.0 %all-gather.13.cloned.1.call-start = ((), (), s32[]{:S(2)}) async-start(), calls=%async_computation.18 | async-start | bytes 5947392 | tf_op jit(solution)/shard_map/all_gather | solution.py:217
  16.1 953.1 %all-gather.15.cloned.1.call-start = ((), (), s32[]{:S(2)}) async-start(), calls=%async_computation.22 | async-start | bytes 2162688 | tf_op jit(solution)/shard_map/all_gather | solution.py:236
  98.1 12.7 collective-permute-start.2
  124.1 14.9 %collective-permute-start = (f32[2,8,128,128]{3,2,1,0:T(8,128)}, f32[2,8,128,128]{3,2,1,0:T(8,128)S(1)}, u32[]{:S(2)}, u32[]{:S(2)}) collective-permute-start(f32[2,8,128,128]{3,2,1,0:T(8,128)} %multiply_add_fusion.28), channel_id=1, source_target_pairs={{0,2},{2,4},{4,6},{6,8},{8,10},{10,12},{12,14},{14,16},{16,18},{18... | collective-permute-start | bytes 3145736 | tf_op jit(solution)/shard_map/while/body/eval_jaxpr/ppermute | solution.py:25
  140.2 18.2 %collective-permute-start = (f32[2,8,128,128]{3,2,1,0:T(8,128)}, f32[2,8,128,128]{3,2,1,0:T(8,128)S(1)}, u32[]{:S(2)}, u32[]{:S(2)}) collective-permute-start(f32[2,8,128,128]{3,2,1,0:T(8,128)} %multiply_add_fusion.28), channel_id=1, source_target_pairs={{0,2},{2,4},{4,6},{6,8},{8,10},{10,12},{12,14},{14,16},{16,18},{18... | collective-permute-start | bytes 3145736 | tf_op jit(solution)/shard_map/while/body/eval_jaxpr/ppermute | solution.py:25
  159.6 18.9 %collective-permute-start = (f32[2,8,128,128]{3,2,1,0:T(8,128)}, f32[2,8,128,128]{3,2,1,0:T(8,128)S(1)}, u32[]{:S(2)}, u32[]{:S(2)}) collective-permute-start(f32[2,8,128,128]{3,2,1,0:T(8,128)} %multiply_add_fusion.28), channel_id=1, source_target_pairs={{0,2},{2,4},{4,6},{6,8},{8,10},{10,12},{12,14},{14,16},{16,18},{18... | collective-permute-start | bytes 3145736 | tf_op jit(solution)/shard_map/while/body/eval_jaxpr/ppermute | solution.py:25
  179.6 26.6 %collective-permute-start = (f32[2,8,128,128]{3,2,1,0:T(8,128)}, f32[2,8,128,128]{3,2,1,0:T(8,128)S(1)}, u32[]{:S(2)}, u32[]{:S(2)}) collective-permute-start(f32[2,8,128,128]{3,2,1,0:T(8,128)} %multiply_add_fusion.28), channel_id=1, source_target_pairs={{0,2},{2,4},{4,6},{6,8},{8,10},{10,12},{12,14},{14,16},{16,18},{18... | collective-permute-start | bytes 3145736 | tf_op jit(solution)/shard_map/while/body/eval_jaxpr/ppermute | solution.py:25
  207.4 19.2 %collective-permute-start = (f32[2,8,128,128]{3,2,1,0:T(8,128)}, f32[2,8,128,128]{3,2,1,0:T(8,128)S(1)}, u32[]{:S(2)}, u32[]{:S(2)}) collective-permute-start(f32[2,8,128,128]{3,2,1,0:T(8,128)} %multiply_add_fusion.28), channel_id=1, source_target_pairs={{0,2},{2,4},{4,6},{6,8},{8,10},{10,12},{12,14},{14,16},{16,18},{18... | collective-permute-start | bytes 3145736 | tf_op jit(solution)/shard_map/while/body/eval_jaxpr/ppermute | solution.py:25
  227.8 27.7 %collective-permute-start = (f32[2,8,128,128]{3,2,1,0:T(8,128)}, f32[2,8,128,128]{3,2,1,0:T(8,128)S(1)}, u32[]{:S(2)}, u32[]{:S(2)}) collective-permute-start(f32[2,8,128,128]{3,2,1,0:T(8,128)} %multiply_add_fusion.28), channel_id=1, source_target_pairs={{0,2},{2,4},{4,6},{6,8},{8,10},{10,12},{12,14},{14,16},{16,18},{18... | collective-permute-start | bytes 3145736 | tf_op jit(solution)/shard_map/while/body/eval_jaxpr/ppermute | solution.py:25
  256.7 23.9 %collective-permute-start = (f32[2,8,128,128]{3,2,1,0:T(8,128)}, f32[2,8,128,128]{3,2,1,0:T(8,128)S(1)}, u32[]{:S(2)}, u32[]{:S(2)}) collective-permute-start(f32[2,8,128,128]{3,2,1,0:T(8,128)} %multiply_add_fusion.28), channel_id=1, source_target_pairs={{0,2},{2,4},{4,6},{6,8},{8,10},{10,12},{12,14},{14,16},{16,18},{18... | collective-permute-start | bytes 3145736 | tf_op jit(solution)/shard_map/while/body/eval_jaxpr/ppermute | solution.py:25
  281.8 18.7 %collective-permute-start = (f32[2,8,128,128]{3,2,1,0:T(8,128)}, f32[2,8,128,128]{3,2,1,0:T(8,128)S(1)}, u32[]{:S(2)}, u32[]{:S(2)}) collective-permute-start(f32[2,8,128,128]{3,2,1,0:T(8,128)} %multiply_add_fusion.28), channel_id=1, source_target_pairs={{0,2},{2,4},{4,6},{6,8},{8,10},{10,12},{12,14},{14,16},{16,18},{18... | collective-permute-start | bytes 3145736 | tf_op jit(solution)/shard_map/while/body/eval_jaxpr/ppermute | solution.py:25
  301.7 19.6 %collective-permute-start = (f32[2,8,128,128]{3,2,1,0:T(8,128)}, f32[2,8,128,128]{3,2,1,0:T(8,128)S(1)}, u32[]{:S(2)}, u32[]{:S(2)}) collective-permute-start(f32[2,8,128,128]{3,2,1,0:T(8,128)} %multiply_add_fusion.28), channel_id=1, source_target_pairs={{0,2},{2,4},{4,6},{6,8},{8,10},{10,12},{12,14},{14,16},{16,18},{18... | collective-permute-start | bytes 3145736 | tf_op jit(solution)/shard_map/while/body/eval_jaxpr/ppermute | solution.py:25
  322.4 18.6 %collective-permute-start = (f32[2,8,128,128]{3,2,1,0:T(8,128)}, f32[2,8,128,128]{3,2,1,0:T(8,128)S(1)}, u32[]{:S(2)}, u32[]{:S(2)}) collective-permute-start(f32[2,8,128,128]{3,2,1,0:T(8,128)} %multiply_add_fusion.28), channel_id=1, source_target_pairs={{0,2},{2,4},{4,6},{6,8},{8,10},{10,12},{12,14},{14,16},{16,18},{18... | collective-permute-start | bytes 3145736 | tf_op jit(solution)/shard_map/while/body/eval_jaxpr/ppermute | solution.py:25
  342.2 25.6 %collective-permute-start = (f32[2,8,128,128]{3,2,1,0:T(8,128)}, f32[2,8,128,128]{3,2,1,0:T(8,128)S(1)}, u32[]{:S(2)}, u32[]{:S(2)}) collective-permute-start(f32[2,8,128,128]{3,2,1,0:T(8,128)} %multiply_add_fusion.28), channel_id=1, source_target_pairs={{0,2},{2,4},{4,6},{6,8},{8,10},{10,12},{12,14},{14,16},{16,18},{18... | collective-permute-start | bytes 3145736 | tf_op jit(solution)/shard_map/while/body/eval_jaxpr/ppermute | solution.py:25
  369.0 17.2 %collective-permute-start = (f32[2,8,128,128]{3,2,1,0:T(8,128)}, f32[2,8,128,128]{3,2,1,0:T(8,128)S(1)}, u32[]{:S(2)}, u32[]{:S(2)}) collective-permute-start(f32[2,8,128,128]{3,2,1,0:T(8,128)} %multiply_add_fusion.28), channel_id=1, source_target_pairs={{0,2},{2,4},{4,6},{6,8},{8,10},{10,12},{12,14},{14,16},{16,18},{18... | collective-permute-start | bytes 3145736 | tf_op jit(solution)/shard_map/while/body/eval_jaxpr/ppermute | solution.py:25
  387.4 17.2 %collective-permute-start = (f32[2,8,128,128]{3,2,1,0:T(8,128)}, f32[2,8,128,128]{3,2,1,0:T(8,128)S(1)}, u32[]{:S(2)}, u32[]{:S(2)}) collective-permute-start(f32[2,8,128,128]{3,2,1,0:T(8,128)} %multiply_add_fusion.28), channel_id=1, source_target_pairs={{0,2},{2,4},{4,6},{6,8},{8,10},{10,12},{12,14},{14,16},{16,18},{18... | collective-permute-start | bytes 3145736 | tf_op jit(solution)/shard_map/while/body/eval_jaxpr/ppermute | solution.py:25
  405.8 17.2 %collective-permute-start = (f32[2,8,128,128]{3,2,1,0:T(8,128)}, f32[2,8,128,128]{3,2,1,0:T(8,128)S(1)}, u32[]{:S(2)}, u32[]{:S(2)}) collective-permute-start(f32[2,8,128,128]{3,2,1,0:T(8,128)} %multiply_add_fusion.28), channel_id=1, source_target_pairs={{0,2},{2,4},{4,6},{6,8},{8,10},{10,12},{12,14},{14,16},{16,18},{18... | collective-permute-start | bytes 3145736 | tf_op jit(solution)/shard_map/while/body/eval_jaxpr/ppermute | solution.py:25
  585.5 16.1 %collective-permute-start.1 = (f32[2,8,128,128]{3,2,1,0:T(8,128)}, f32[2,8,128,128]{3,2,1,0:T(8,128)}, u32[]{:S(2)}, u32[]{:S(2)}) collective-permute-start(f32[2,8,128,128]{3,2,1,0:T(8,128)} %multiply_add_fusion.29), channel_id=1, source_target_pairs={{2,0},{4,2},{6,4},{8,6},{10,8},{12,10},{14,12},{16,14},{18,16},{20... | collective-permute-start | bytes 3145736 | tf_op jit(solution)/shard_map/while/body/eval_jaxpr/ppermute | solution.py:25
  604.3 19.1 %collective-permute-start.1 = (f32[2,8,128,128]{3,2,1,0:T(8,128)}, f32[2,8,128,128]{3,2,1,0:T(8,128)}, u32[]{:S(2)}, u32[]{:S(2)}) collective-permute-start(f32[2,8,128,128]{3,2,1,0:T(8,128)} %multiply_add_fusion.29), channel_id=1, source_target_pairs={{2,0},{4,2},{6,4},{8,6},{10,8},{12,10},{14,12},{16,14},{18,16},{20... | collective-permute-start | bytes 3145736 | tf_op jit(solution)/shard_map/while/body/eval_jaxpr/ppermute | solution.py:25
  626.1 16.4 %collective-permute-start.1 = (f32[2,8,128,128]{3,2,1,0:T(8,128)}, f32[2,8,128,128]{3,2,1,0:T(8,128)}, u32[]{:S(2)}, u32[]{:S(2)}) collective-permute-start(f32[2,8,128,128]{3,2,1,0:T(8,128)} %multiply_add_fusion.29), channel_id=1, source_target_pairs={{2,0},{4,2},{6,4},{8,6},{10,8},{12,10},{14,12},{16,14},{18,16},{20... | collective-permute-start | bytes 3145736 | tf_op jit(solution)/shard_map/while/body/eval_jaxpr/ppermute | solution.py:25
  645.3 18.8 %collective-permute-start.1 = (f32[2,8,128,128]{3,2,1,0:T(8,128)}, f32[2,8,128,128]{3,2,1,0:T(8,128)}, u32[]{:S(2)}, u32[]{:S(2)}) collective-permute-start(f32[2,8,128,128]{3,2,1,0:T(8,128)} %multiply_add_fusion.29), channel_id=1, source_target_pairs={{2,0},{4,2},{6,4},{8,6},{10,8},{12,10},{14,12},{16,14},{18,16},{20... | collective-permute-start | bytes 3145736 | tf_op jit(solution)/shard_map/while/body/eval_jaxpr/ppermute | solution.py:25
  666.7 17.3 %collective-permute-start.1 = (f32[2,8,128,128]{3,2,1,0:T(8,128)}, f32[2,8,128,128]{3,2,1,0:T(8,128)}, u32[]{:S(2)}, u32[]{:S(2)}) collective-permute-start(f32[2,8,128,128]{3,2,1,0:T(8,128)} %multiply_add_fusion.29), channel_id=1, source_target_pairs={{2,0},{4,2},{6,4},{8,6},{10,8},{12,10},{14,12},{16,14},{18,16},{20... | collective-permute-start | bytes 3145736 | tf_op jit(solution)/shard_map/while/body/eval_jaxpr/ppermute | solution.py:25
  686.8 17.3 %collective-permute-start.1 = (f32[2,8,128,128]{3,2,1,0:T(8,128)}, f32[2,8,128,128]{3,2,1,0:T(8,128)}, u32[]{:S(2)}, u32[]{:S(2)}) collective-permute-start(f32[2,8,128,128]{3,2,1,0:T(8,128)} %multiply_add_fusion.29), channel_id=1, source_target_pairs={{2,0},{4,2},{6,4},{8,6},{10,8},{12,10},{14,12},{16,14},{18,16},{20... | collective-permute-start | bytes 3145736 | tf_op jit(solution)/shard_map/while/body/eval_jaxpr/ppermute | solution.py:25
  706.8 17.3 %collective-permute-start.1 = (f32[2,8,128,128]{3,2,1,0:T(8,128)}, f32[2,8,128,128]{3,2,1,0:T(8,128)}, u32[]{:S(2)}, u32[]{:S(2)}) collective-permute-start(f32[2,8,128,128]{3,2,1,0:T(8,128)} %multiply_add_fusion.29), channel_id=1, source_target_pairs={{2,0},{4,2},{6,4},{8,6},{10,8},{12,10},{14,12},{16,14},{18,16},{20... | collective-permute-start | bytes 3145736 | tf_op jit(solution)/shard_map/while/body/eval_jaxpr/ppermute | solution.py:25
  726.8 17.3 %collective-permute-start.1 = (f32[2,8,128,128]{3,2,1,0:T(8,128)}, f32[2,8,128,128]{3,2,1,0:T(8,128)}, u32[]{:S(2)}, u32[]{:S(2)}) collective-permute-start(f32[2,8,128,128]{3,2,1,0:T(8,128)} %multiply_add_fusion.29), channel_id=1, source_target_pairs={{2,0},{4,2},{6,4},{8,6},{10,8},{12,10},{14,12},{16,14},{18,16},{20... | collective-permute-start | bytes 3145736 | tf_op jit(solution)/shard_map/while/body/eval_jaxpr/ppermute | solution.py:25
  746.9 17.3 %collective-permute-start.1 = (f32[2,8,128,128]{3,2,1,0:T(8,128)}, f32[2,8,128,128]{3,2,1,0:T(8,128)}, u32[]{:S(2)}, u32[]{:S(2)}) collective-permute-start(f32[2,8,128,128]{3,2,1,0:T(8,128)} %multiply_add_fusion.29), channel_id=1, source_target_pairs={{2,0},{4,2},{6,4},{8,6},{10,8},{12,10},{14,12},{16,14},{18,16},{20... | collective-permute-start | bytes 3145736 | tf_op jit(solution)/shard_map/while/body/eval_jaxpr/ppermute | solution.py:25
  766.9 17.3 %collective-permute-start.1 = (f32[2,8,128,128]{3,2,1,0:T(8,128)}, f32[2,8,128,128]{3,2,1,0:T(8,128)}, u32[]{:S(2)}, u32[]{:S(2)}) collective-permute-start(f32[2,8,128,128]{3,2,1,0:T(8,128)} %multiply_add_fusion.29), channel_id=1, source_target_pairs={{2,0},{4,2},{6,4},{8,6},{10,8},{12,10},{14,12},{16,14},{18,16},{20... | collective-permute-start | bytes 3145736 | tf_op jit(solution)/shard_map/while/body/eval_jaxpr/ppermute | solution.py:25
  787.0 17.3 %collective-permute-start.1 = (f32[2,8,128,128]{3,2,1,0:T(8,128)}, f32[2,8,128,128]{3,2,1,0:T(8,128)}, u32[]{:S(2)}, u32[]{:S(2)}) collective-permute-start(f32[2,8,128,128]{3,2,1,0:T(8,128)} %multiply_add_fusion.29), channel_id=1, source_target_pairs={{2,0},{4,2},{6,4},{8,6},{10,8},{12,10},{14,12},{16,14},{18,16},{20... | collective-permute-start | bytes 3145736 | tf_op jit(solution)/shard_map/while/body/eval_jaxpr/ppermute | solution.py:25
  807.0 17.3 %collective-permute-start.1 = (f32[2,8,128,128]{3,2,1,0:T(8,128)}, f32[2,8,128,128]{3,2,1,0:T(8,128)}, u32[]{:S(2)}, u32[]{:S(2)}) collective-permute-start(f32[2,8,128,128]{3,2,1,0:T(8,128)} %multiply_add_fusion.29), channel_id=1, source_target_pairs={{2,0},{4,2},{6,4},{8,6},{10,8},{12,10},{14,12},{16,14},{18,16},{20... | collective-permute-start | bytes 3145736 | tf_op jit(solution)/shard_map/while/body/eval_jaxpr/ppermute | solution.py:25
  827.0 17.3 %collective-permute-start.1 = (f32[2,8,128,128]{3,2,1,0:T(8,128)}, f32[2,8,128,128]{3,2,1,0:T(8,128)}, u32[]{:S(2)}, u32[]{:S(2)}) collective-permute-start(f32[2,8,128,128]{3,2,1,0:T(8,128)} %multiply_add_fusion.29), channel_id=1, source_target_pairs={{2,0},{4,2},{6,4},{8,6},{10,8},{12,10},{14,12},{16,14},{18,16},{20... | collective-permute-start | bytes 3145736 | tf_op jit(solution)/shard_map/while/body/eval_jaxpr/ppermute | solution.py:25
  847.1 17.3 %collective-permute-start.1 = (f32[2,8,128,128]{3,2,1,0:T(8,128)}, f32[2,8,128,128]{3,2,1,0:T(8,128)}, u32[]{:S(2)}, u32[]{:S(2)}) collective-permute-start(f32[2,8,128,128]{3,2,1,0:T(8,128)} %multiply_add_fusion.29), channel_id=1, source_target_pairs={{2,0},{4,2},{6,4},{8,6},{10,8},{12,10},{14,12},{16,14},{18,16},{20... | collective-permute-start | bytes 3145736 | tf_op jit(solution)/shard_map/while/body/eval_jaxpr/ppermute | solution.py:25
  867.1 17.3 %collective-permute-start.1 = (f32[2,8,128,128]{3,2,1,0:T(8,128)}, f32[2,8,128,128]{3,2,1,0:T(8,128)}, u32[]{:S(2)}, u32[]{:S(2)}) collective-permute-start(f32[2,8,128,128]{3,2,1,0:T(8,128)} %multiply_add_fusion.29), channel_id=1, source_target_pairs={{2,0},{4,2},{6,4},{8,6},{10,8},{12,10},{14,12},{16,14},{18,16},{20... | collective-permute-start | bytes 3145736 | tf_op jit(solution)/shard_map/while/body/eval_jaxpr/ppermute | solution.py:25
  906.0 10.7 all-to-all-start.2
  916.7 9.4 all-to-all-start.4
  920.8 154.3 %reduce-scatter.16.cloned.1.call-start = ((), (), s32[]{:S(2)}) async-start(), calls=%async_computation.24 | async-start | bytes 557056
  922.7 171.0 %reduce-scatter.10.cloned.1.call-start = ((), (), s32[]{:S(2)}) async-start(), calls=%async_computation.20 | async-start | bytes 2228224 | tf_op jit(solution)/shard_map/reduce_scatter | solution.py:295
  928.9 249.2 %reduce-scatter.14.cloned.1.call-start = ((), (), s32[]{:S(2)}) async-start(), calls=%async_computation.23 | async-start | bytes 6127616 | tf_op jit(solution)/shard_map/reduce_scatter | solution.py:297
  973.9 312.2 %reduce-scatter.8.cloned.1.call-start = ((), (), s32[]{:S(2)}) async-start(), calls=%async_computation.19 | async-start | bytes 8912896 | tf_op jit(solution)/shard_map/reduce_scatter | solution.py:293
  1035.4 28.0 %all-to-all-start.6 = ((bf16[128,2,2816]{2,0,1:T(8,128)(2,1)}), bf16[128,2,2816]{2,0,1:T(8,128)(2,1)S(1)}, u32[]{:S(2)}, u32[]{:S(2)}) async-start(bf16[128,2,2816]{2,0,1:T(8,128)(2,1)} %bitcast.1133), calls=%async_computation.8 | async-start | bytes 2883584 | tf_op jit(solution)/shard_map/all_to_all | solution.py:281
  1039.2 376.9 %reduce-scatter.12.cloned.1.call-start = ((), (), s32[]{:S(2)}) async-start(), calls=%async_computation.21 | async-start | bytes 12255232 | tf_op jit(solution)/shard_map/reduce_scatter | solution.py:296
  1093.7 7.8 all-to-all-start.5
  1178.2 9.4 all-to-all-start.9
  1286.2 11.8 all-to-all-start.1
  1416.1 52.1 %all-to-all-start.7 = ((f32[2,32,2816]{2,1,0:T(8,128)}), f32[2,32,2816]{2,1,0:T(8,128)S(1)}, u32[]{:S(2)}, u32[]{:S(2)}) async-start(f32[2,32,2816]{2,1,0:T(8,128)} %bitcast.1153), calls=%async_computation.10 | async-start | bytes 1441792 | tf_op jit(solution)/shard_map/all_to_all | solution.py:303
  (313 other events, 3946.7 us)
Sparse Core Ops, SparseCore 0:
  11.2 80.8 all-gather.6
  95.2 57.6 all-gather.8
  155.7 107.6 all-gather.10
  266.2 72.4 all-gather.12
  903.4 65.6 all-gather.14
  972.5 56.2 reduce-scatter.15
  1033.1 60.6 reduce-scatter.9
  1097.6 80.4 reduce-scatter.13
  1182.2 103.8 reduce-scatter.7
  1290.1 125.9 reduce-scatter.11
where the time goes:
time: 1490 us; the launch traced here: 1480 us
  waiting for transfers between devices  627 us (42%)
  starting transfers between devices  307 us (21%)
  matrix products  190 us (13%)
  blocking collectives  172 us (12%)
  other arithmetic  107 us (7%)
  local copies, waits for them, and re-layouts  52.2 us (4%)
  between operations  20.3 us (1%)
    ppermute x32, waiting for transfers between devices, passed_along(): lax.ppermute(value, axis, [(source, source + steps) for source in range(l...  278 us
    ppermute x32, starting transfers between devices, passed_along(): lax.ppermute(value, axis, [(source, source + steps) for source in range(l...  274 us
    reduce_scatter x1, waiting for transfers between devices, per_device(): lax.psum_scatter(part_up, 'grp', scatter_dimension=0, tiled=True)  118 us
    reduce_scatter x1, waiting for transfers between devices, per_device(): lax.psum_scatter(part_in, 'grp', scatter_dimension=0, tiled=True)  98.6 us
    reduce_scatter x1, waiting for transfers between devices, per_device(): lax.psum_scatter(part_down, 'grp', scatter_dimension=0, tiled=True)  76.6 us
    all_gather x1, blocking collectives, per_device(): lax.all_gather(proj_gates, ('grp', 'narrow'), axis=0, tiled=True)  71.2 us
    psum x1, blocking collectives, per_device(): lax.psum((grad_conv_taps, grad_attn_norm, grad_out_norm, grad_ffn_norm, g...  42.2 us
    add x15, other arithmetic, relay_backward(): grad_incoming + scale_state(through, later_grad)  40.7 us
  transfers between devices with their start and end apart: 51, of which 40 were waited for; matrix products, arithmetic and copies ran while one was open for 12% of the time, Pallas kernels for 0%

commit v1 on v0

v1 whole, which is shorter than its diff:
```python
import functools

import jax
import jax.numpy as jnp
from jax import lax
from jax.sharding import Mesh, PartitionSpec as P

D = 1024
HEADS = 8
HEAD_DIM = 128
FF = 2816
CONV = 4
CG_STEPS = 8

EPSILON = 1e-06
CG_EPSILON = 1e-06
REGULARIZER = 16.0
PRECISE = lax.Precision.HIGHEST
EVERY = ("out", "inn", "narrow")
BF = jnp.bfloat16
F32 = jnp.float32


def xor_permute(value, axis, distance):
    count = lax.axis_size(axis)
    return lax.ppermute(value, axis, [(source, source ^ distance) for source in range(count)])


def passed_along(value, steps):
    count = lax.axis_size("out")
    leading, last = (max(0, -steps), min(count, count - steps))
    return lax.ppermute(value, "out", [(source, source + steps) for source in range(leading, last)])


def butterfly_sum(value):
    for axis in EVERY:
        distance = 1
        while distance < lax.axis_size(axis):
            value = value + xor_permute(value, axis, distance)
            distance *= 2
    return value


def gather_pieces(mine):
    pieces = {0: mine, 1: xor_permute(mine, "inn", 1)}
    for distance in (2, 4, 6):
        pieces[distance] = xor_permute(mine, "inn", distance)
    for distance in (2, 4, 6):
        pieces[distance + 1] = xor_permute(pieces[distance], "inn", 1)
    return [pieces[k] for k in range(8)]


def gather_rows(mine):
    pieces = jnp.stack(gather_pieces(mine))
    order = jnp.arange(8, dtype=jnp.int32) ^ lax.axis_index("inn")
    return pieces[order].reshape((8 * mine.shape[0],) + mine.shape[1:])


def scatter_sum(parts):
    low = parts.astype(BF)
    me = lax.axis_index("inn")

    def block(k):
        return lax.dynamic_index_in_dim(low, me ^ k, 0, keepdims=False)

    paired = {
        k: block(k).astype(F32) + xor_permute(block(k + 1), "inn", 1).astype(F32) for k in (0, 2, 4, 6)
    }
    total = paired[0]
    for k in (2, 4, 6):
        total = total + xor_permute(paired[k].astype(BF), "inn", k).astype(F32)
    return total


def exchange(blocks, axes):
    return lax.all_to_all(blocks, axes, split_axis=0, concat_axis=0, tiled=True)


def rms_norm(values, norm_gain):
    return (
        values * lax.rsqrt(jnp.mean(values * values, axis=-1, keepdims=True) + EPSILON) * norm_gain
    )


def unit_rows(rows):
    return rows * lax.rsqrt(jnp.sum(rows * rows, axis=-1, keepdims=True) + EPSILON)


def conv_features(extended, conv_taps, place_docs):
    length = extended.shape[0] - (CONV - 1)
    own_docs = place_docs[CONV - 1 :]
    summed = jnp.zeros((length, extended.shape[1]), F32)
    for offset in range(CONV):
        first_row = CONV - 1 - offset
        window = extended[first_row : first_row + length]
        same_doc = (place_docs[first_row : first_row + length] == own_docs).astype(F32)
        summed = summed + conv_taps[offset] * window * same_doc[:, None]
    activated = jax.nn.silu(summed)
    return (
        unit_rows(activated[:, :HEAD_DIM]),
        unit_rows(activated[:, HEAD_DIM : 2 * HEAD_DIM]),
        activated[:, 2 * HEAD_DIM :],
    )


def gate_values(gate_logits, decay_log):
    log_decay = -jnp.exp(decay_log) * jax.nn.sigmoid(gate_logits[:, 0])
    return (log_decay, jax.nn.sigmoid(gate_logits[:, 1]))


def decay_tables(log_decay, segments, carry_flags):
    cumulative = jnp.cumsum(log_decay, axis=1)
    length = segments.shape[1]
    position = jnp.arange(length, dtype=jnp.int32)
    visible = (segments[:, :, None] == segments[:, None, :]) & (
        position[None, :] <= position[:, None]
    )[None]
    spread = jnp.exp(jnp.minimum(cumulative[:, :, None] - cumulative[:, None, :], 0.0)) * visible.astype(
        F32
    )
    carried = ((segments == segments[:, :1]) & carry_flags[:, None]).astype(F32)
    entry_decay = jnp.exp(cumulative) * carried
    last_doc = (segments == segments[:, length - 1 :]).astype(F32)
    tail_decay = jnp.exp(cumulative[:, length - 1 :] - cumulative) * last_doc
    return (spread, entry_decay, tail_decay)


def ein(spec, *operands):
    return jnp.einsum(spec, *operands, precision=PRECISE)


def apply_system(probe_rows, keys, weights, entry_decay, curvature):
    carried_part = ein("hck,hkl->hcl", probe_rows, curvature) * entry_decay[:, :, None]
    scores = ein("hck,hjk->hcj", probe_rows, keys) * weights
    return REGULARIZER * probe_rows + carried_part + ein("hcj,hjk->hck", scores, keys)


def block_out(queries, keys, values, log_decay, in_gate, state_in, segments, carry_flags):
    spread, entry_decay, tail_decay = decay_tables(log_decay, segments, carry_flags)
    weights = spread * in_gate[:, None, :]
    solution = jnp.zeros_like(queries)
    residual = queries
    direction = queries
    norm_now = jnp.sum(residual * residual, axis=-1, keepdims=True)
    for iteration in range(CG_STEPS):
        applied = apply_system(direction, keys, weights, entry_decay, state_in[0])
        step_size = norm_now / (jnp.sum(direction * applied, axis=-1, keepdims=True) + CG_EPSILON)
        solution = solution + step_size * direction
        residual = residual - step_size * applied
        if iteration + 1 < CG_STEPS:
            norm_next = jnp.sum(residual * residual, axis=-1, keepdims=True)
            direction = residual + norm_next / (norm_now + CG_EPSILON) * direction
            norm_now = norm_next
    carried_part = ein("hck,hvk->hcv", solution, state_in[1]) * entry_decay[:, :, None]
    scores = ein("hck,hjk->hcj", solution, keys) * weights
    return carried_part + ein("hcj,hjv->hcv", scores, values)


def block_summary(keys, values, log_decay, in_gate, segments, carry_flags):
    spread, entry_decay, tail_decay = decay_tables(log_decay, segments, carry_flags)
    deposit = tail_decay * in_gate
    curvature = ein("hc,hck,hcl->hkl", deposit, keys, keys)
    coupling = ein("hc,hcv,hck->hvk", deposit, values, keys)
    return (entry_decay[:, -1], jnp.stack([curvature, coupling]))


def out_gate(mesa_out, pre_gate, out_norm):
    normed = mesa_out * lax.rsqrt(jnp.mean(mesa_out * mesa_out, axis=-1, keepdims=True) + EPSILON)
    return normed * out_norm * jax.nn.silu(pre_gate)


def swiglu(gate_up):
    half = gate_up.shape[1] // 2
    return jax.nn.silu(gate_up[:, :half]) * gate_up[:, half:]


def dot32(left, right):
    return jnp.dot(left, right, preferred_element_type=F32)


def per_device(
    block_input,
    proj_in,
    proj_gates,
    proj_out,
    ffn_up,
    ffn_down,
    conv_taps,
    attn_norm,
    out_norm,
    ffn_norm,
    decay_log,
    doc_lengths,
    cotangent,
):
    outer = lax.axis_size("out")
    narrow = lax.axis_size("narrow")
    devices = outer * 8 * narrow
    me = lax.axis_index("inn")
    token_count = block_input.shape[1]
    group_tokens = 8 * token_count
    in_rows = proj_in.shape[0]
    units = ffn_down.shape[0]
    own_units = outer * narrow * units

    doc_ends = jnp.cumsum(doc_lengths[0])
    places = (
        lax.axis_index("out") * group_tokens
        - (CONV - 1)
        + jnp.arange(group_tokens + CONV - 1, dtype=jnp.int32)
    )
    counted = jnp.sum((places[:, None] >= doc_ends[None, :]).astype(jnp.int32), axis=1)
    place_docs = jnp.where(places >= 0, counted, -1)
    segments = place_docs[CONV - 1 :].reshape(8, token_count)
    carry_flags = segments[:, 0] == place_docs[CONV - 2 : -1].reshape(8, token_count)[:, 0]

    def for_heads(blocks):
        spread_out = jnp.broadcast_to(
            blocks[None, :, None], (outer, 8, narrow) + blocks.shape[1:]
        )
        return spread_out.reshape((devices,) + blocks.shape[1:])

    in_blocks = proj_in.reshape(in_rows, 4, 8, HEAD_DIM).transpose(2, 0, 1, 3)
    in_blocks = in_blocks.reshape(8, in_rows, 4 * HEAD_DIM)
    gate_blocks = proj_gates.reshape(in_rows, 2, 8).transpose(2, 0, 1)
    gate_blocks = jnp.pad(gate_blocks, ((0, 0), (0, 0), (0, HEAD_DIM - 2)))
    in_mine = exchange(for_heads(jnp.concatenate([in_blocks, gate_blocks], axis=2)), EVERY)
    in_mine = in_mine.reshape(D, 5 * HEAD_DIM)

    hidden_in = block_input[0].astype(F32)
    normed, norm_one_pull = jax.vjp(rms_norm, hidden_in, attn_norm)
    normed_all = gather_rows(normed.astype(BF))

    up_blocks = ffn_up.reshape(in_rows, 2, outer, 8, narrow, units).transpose(3, 0, 1, 2, 4, 5)
    up_mine = exchange(for_heads(up_blocks.reshape(8, in_rows, 2 * own_units)), EVERY)
    up_mine = up_mine.reshape(D, 2 * own_units)
    down_mine = lax.all_gather(ffn_down, ("out", "narrow"), axis=0, tiled=True)
    out_full = lax.all_gather(proj_out, EVERY, axis=0, tiled=True)
    grad_output = cotangent[0]
    grad_output_all = gather_rows(grad_output)

    projected = dot32(normed_all, in_mine)
    features = projected[:, : 3 * HEAD_DIM]
    pre_gate = projected[:, 3 * HEAD_DIM : 4 * HEAD_DIM]
    gate_logits = projected[:, 4 * HEAD_DIM : 4 * HEAD_DIM + 2]
    before_rows = passed_along(features[group_tokens - (CONV - 1) :], 1)
    extended = jnp.concatenate([before_rows, features], axis=0)
    own_taps = lax.dynamic_index_in_dim(
        conv_taps.reshape(CONV, 3, 8, HEAD_DIM), me, 2, keepdims=False
    ).reshape(CONV, 3 * HEAD_DIM)
    own_out_norm = lax.dynamic_slice_in_dim(out_norm, me * HEAD_DIM, HEAD_DIM)
    (queries, key_rows, value_rows), conv_pull = jax.vjp(
        functools.partial(conv_features, place_docs=place_docs), extended, own_taps
    )
    own_decay = lax.dynamic_index_in_dim(decay_log, me, 0, keepdims=False)
    (log_decay, in_gate), gate_pull = jax.vjp(gate_values, gate_logits, own_decay)

    def chunked(rows):
        return rows.reshape((8, token_count) + rows.shape[1:])

    queries, key_rows, value_rows, log_decay, in_gate = (
        chunked(queries),
        chunked(key_rows),
        chunked(value_rows),
        chunked(log_decay),
        chunked(in_gate),
    )
    tables = dict(segments=segments, carry_flags=carry_flags)
    (through, fresh), summary_pull = jax.vjp(
        functools.partial(block_summary, **tables), key_rows, value_rows, log_decay, in_gate
    )
    states = [jnp.zeros_like(fresh[:, 0])]
    reach = [jnp.ones((), F32)]
    for chunk in range(8):
        states.append(through[chunk] * states[-1] + fresh[:, chunk])
        reach.append(through[chunk] * reach[-1])
    arriving = jnp.zeros_like(states[0])
    for relay in range(outer - 1):
        arriving = passed_along(reach[8] * arriving + states[8], 1)
    incoming = jnp.stack([states[c] + reach[c] * arriving for c in range(8)], axis=1)
    mesa_out, out_pull = jax.vjp(
        functools.partial(block_out, **tables),
        queries,
        key_rows,
        value_rows,
        log_decay,
        in_gate,
        incoming,
    )
    gated_head, gate_out_pull = jax.vjp(
        out_gate, mesa_out.reshape(group_tokens, HEAD_DIM), pre_gate, own_out_norm
    )
    gated_low = lax.all_to_all(
        gated_head.astype(BF), "inn", split_axis=0, concat_axis=1, tiled=True
    )
    hidden = hidden_in + dot32(gated_low, out_full)
    normed_two, norm_two_pull = jax.vjp(rms_norm, hidden, ffn_norm)
    normed_two_all = gather_rows(normed_two.astype(BF))
    gate_up = dot32(normed_two_all, up_mine)
    activated, swiglu_pull = jax.vjp(swiglu, gate_up)
    act_low = activated.astype(BF)
    grad_act = dot32(grad_output_all, down_mine.T)
    (grad_gate_up,) = swiglu_pull(grad_act)
    grad_gate_low = grad_gate_up.astype(BF)
    grad_normed_two = scatter_sum(
        dot32(grad_gate_low, up_mine.T).reshape(8, token_count, D)
    )
    block_output = hidden + scatter_sum(dot32(act_low, down_mine).reshape(8, token_count, D))
    grad_hidden_norm, grad_ffn_norm = norm_two_pull(grad_normed_two)
    grad_hidden = grad_output.astype(F32) + grad_hidden_norm
    grad_branch = grad_hidden.astype(BF)
    grad_gated = dot32(grad_branch, out_full.T)
    grad_gated_head = lax.all_to_all(
        grad_gated.astype(BF), "inn", split_axis=1, concat_axis=0, tiled=True
    ).astype(F32)

    def owners_sum(parts):
        columns = parts.shape[1]
        received = exchange(parts.astype(BF).reshape(devices, in_rows, columns), EVERY)
        received = received.reshape(outer, 8, narrow, in_rows, columns)
        return jnp.sum(received.astype(F32), axis=(0, 2))

    up_sum = owners_sum(dot32(normed_two_all.T, grad_gate_low))
    grad_up = (
        up_sum.reshape(8, in_rows, 2, outer, narrow, units)
        .transpose(1, 2, 3, 0, 4, 5)
        .reshape(in_rows, 2 * FF)
    )
    down_parts = dot32(act_low.T, grad_output_all).astype(BF).reshape(outer * narrow, units, D)
    grad_down = jnp.sum(exchange(down_parts, ("out", "narrow")).astype(F32), axis=0)
    out_parts = dot32(gated_low.T, grad_branch).astype(BF).reshape(devices, in_rows, D)
    grad_out = jnp.sum(exchange(out_parts, EVERY).astype(F32), axis=0)

    grad_mesa, grad_pre_gate, grad_out_norm = gate_out_pull(grad_gated_head)
    grad_queries, grad_keys_out, grad_values_out, grad_decay_out, grad_gate_out, grad_incoming = (
        out_pull(chunked(grad_mesa))
    )
    later = jnp.zeros_like(arriving)
    for relay in range(outer - 1):
        total = later
        for chunk in reversed(range(8)):
            total = grad_incoming[:, chunk] + through[chunk] * total
        later = passed_along(total, -1)
    after = [later]
    for chunk in reversed(range(1, 8)):
        after.append(grad_incoming[:, chunk] + through[chunk] * after[-1])
    after_grad = jnp.stack(after[::-1], axis=1)
    grad_through = jnp.sum(after_grad * incoming, axis=(0, 2, 3))
    grad_keys_sum, grad_values_sum, grad_decay_sum, grad_gate_sum = summary_pull(
        (grad_through, after_grad)
    )

    def flat(rows):
        return rows.reshape((group_tokens,) + rows.shape[2:])

    grad_logits, grad_decay_log = gate_pull(
        (flat(grad_decay_out + grad_decay_sum), flat(grad_gate_out + grad_gate_sum))
    )
    grad_extended, grad_taps = conv_pull(
        (flat(grad_queries), flat(grad_keys_out + grad_keys_sum), flat(grad_values_out + grad_values_sum))
    )
    returned = passed_along(grad_extended[: CONV - 1], -1)
    grad_features = grad_extended[CONV - 1 :] + jnp.pad(
        returned, ((group_tokens - (CONV - 1), 0), (0, 0))
    )
    grad_projected = jnp.concatenate(
        [
            grad_features,
            grad_pre_gate,
            jnp.pad(grad_logits, ((0, 0), (0, HEAD_DIM - 2))),
        ],
        axis=1,
    ).astype(BF)
    grad_normed = scatter_sum(dot32(grad_projected, in_mine.T).reshape(8, token_count, D))
    grad_input_norm, grad_attn_norm = norm_one_pull(grad_normed)
    input_grad = grad_hidden + grad_input_norm
    in_sum = owners_sum(dot32(normed_all.T, grad_projected))
    grad_in = (
        in_sum[:, :, : 4 * HEAD_DIM]
        .reshape(8, in_rows, 4, HEAD_DIM)
        .transpose(1, 2, 0, 3)
        .reshape(in_rows, 4 * D)
    )
    grad_gates = (
        in_sum[:, :, 4 * HEAD_DIM : 4 * HEAD_DIM + 2].transpose(1, 2, 0).reshape(in_rows, 16)
    )

    own_head = jnp.arange(8, dtype=jnp.int32) == me
    head_parts = jnp.concatenate(
        [grad_taps.reshape(-1), grad_out_norm, jnp.broadcast_to(grad_decay_log, (HEAD_DIM,))]
    )
    head_parts = jnp.where(own_head[:, None], head_parts[None, :], 0.0)
    small = jnp.concatenate([head_parts.reshape(-1, HEAD_DIM), grad_attn_norm.reshape(-1, HEAD_DIM), grad_ffn_norm.reshape(-1, HEAD_DIM)])
    small = butterfly_sum(small)
    heads_rows = small[: 8 * (3 * CONV + 2)].reshape(8, 3 * CONV + 2, HEAD_DIM)
    taps_total = heads_rows[:, : 3 * CONV].reshape(8, CONV, 3, HEAD_DIM).transpose(1, 2, 0, 3)
    return (
        block_output.astype(BF)[None],
        input_grad[None],
        grad_in,
        grad_gates,
        grad_out,
        grad_up,
        grad_down,
        taps_total.reshape(CONV, 3 * D),
        small[8 * (3 * CONV + 2) :][:8].reshape(D),
        heads_rows[:, 3 * CONV].reshape(D),
        small[8 * (3 * CONV + 2) :][8:].reshape(D),
        heads_rows[:, 3 * CONV + 1, 0],
    )


def solution(mesh):
    fine = Mesh(
        mesh.devices.reshape(-1, 8, mesh.shape["narrow"]), EVERY
    )
    tokens = P("narrow", ("out", "inn"), None)
    rows = P(EVERY, None)
    return jax.shard_map(
        per_device,
        mesh=fine,
        in_specs=(tokens, rows, rows, rows, rows, rows)
        + (P(), P(), P(), P(), P())
        + (P("narrow", None), tokens),
        out_specs=(tokens, tokens, rows, rows, rows, rows, rows, P(), P(), P(), P(), P()),
        check_vma=False,
    )
```

time: 1490 us -> 634 us (0.43)
  waiting for transfers between devices: 627 us -> 165 us
  starting transfers between devices: 307 us -> 82.1 us
  blocking collectives: 172 us -> 45.2 us
  matrix products: 190 us -> 149 us
  other arithmetic: 107 us -> 73.4 us
  local copies, waits for them, and re-layouts: 52.2 us -> 82.8 us
    reduce_scatter x4 -> x0, waiting for transfers between devices: 303 us -> none  [the longest x1 118 us: per_device(): lax.psum_scatter(part_up, 'grp', scatter_dimension=0, tiled=True)]
    ppermute x32 -> x51, starting transfers between devices: 274 us -> 41.4 us  [the longest x47 33.8 us: xor_permute(): lax.ppermute(value, axis, [(source, source ^ distance) for source in rang...]
    ppermute x32 -> x51, waiting for transfers between devices: 278 us -> 133 us  [the longest x47 101 us: xor_permute(): lax.ppermute(value, axis, [(source, source ^ distance) for source in rang...]
    all_gather x4 -> x1, blocking collectives: 113 us -> 45.2 us  [per_device(): down_mine = lax.all_gather(ffn_down, ('out', 'narrow'), axis=0, tiled=True)]
    add x32 -> x10, other arithmetic: 58.4 us -> 10.9 us  [the longest x1 4.38 us: per_device(): arriving = passed_along(reach[8] * arriving + states[8], 1)]
    psum x1 -> x0, blocking collectives: 42.2 us -> none  [per_device(): lax.psum((grad_conv_taps, grad_attn_norm, grad_out_norm, grad_ffn_norm, g...]
    dot_general x101 -> x99, matrix products: 188 us -> 149 us  [the longest x87 113 us: ein(): return jnp.einsum(spec, *operands, precision=PRECISE)]
    all_gather x5 -> x1, waiting for transfers between devices: 25.3 us -> 0.02 us  [per_device(): out_full = lax.all_gather(proj_out, EVERY, axis=0, tiled=True)]
  transfers between devices with their start and end apart: 51 -> 60, of which waited for: 40 -> 25; matrix products, arithmetic and copies ran while one was open for 12% -> 44% of each run, Pallas kernels for 0% -> 0%
where the time goes in v1:
time: 634 us; the launch traced here: 623 us
  waiting for transfers between devices  165 us (26%)
  matrix products  149 us (24%)
  local copies, waits for them, and re-layouts  82.8 us (13%)
  starting transfers between devices  82.1 us (13%)
  other arithmetic  73.4 us (12%)
  blocking collectives  45.2 us (7%)
  between operations  25.6 us (4%)
    dot_general x87, matrix products, ein(): return jnp.einsum(spec, *operands, precision=PRECISE)  113 us
    ppermute x47, waiting for transfers between devices, xor_permute(): lax.ppermute(value, axis, [(source, source ^ distance) for source in rang...  101 us
    all_gather x1, blocking collectives, per_device(): down_mine = lax.all_gather(ffn_down, ('out', 'narrow'), axis=0, tiled=True)  45.2 us
    unnamed x383, local copies, waits for them, and re-layouts  38.4 us
    dot_general x12, matrix products, dot32(): return jnp.dot(left, right, preferred_element_type=F32)  36.1 us
    ppermute x47, starting transfers between devices, xor_permute(): lax.ppermute(value, axis, [(source, source ^ distance) for source in rang...  33.8 us
    ppermute x4, waiting for transfers between devices, passed_along(): lax.ppermute(value, 'out', [(source, source + steps) for source in range(...  31.9 us
    all_to_all x6, starting transfers between devices, exchange(): return lax.all_to_all(blocks, axes, split_axis=0, concat_axis=0, tiled=True)  31.3 us
  transfers between devices with their start and end apart: 60, of which 25 were waited for; matrix products, arithmetic and copies ran while one was open for 44% of the time, Pallas kernels for 0%

profile of v1, /device:TPU:0, one launch (start us, length us, event | category | flops | bytes accessed | tf_op | source)
XLA Modules:
  0.0 622.8 jit_solution(16926994156921495322)
XLA Ops:
  17.9 6.4 %all-to-all-start = ((bf16[32,32,640]{2,1,0:T(8,128)(2,1)}), bf16[32,32,640]{2,1,0:T(8,128)(2,1)}, u32[]{:S(2)}, u32[]{:S(2)}) async-start(bf16[32,32,640]{2,1,0:T(8,128)(2,1)} %bitcast.13), calls=%async_computation | async-start | bytes 2621440 | tf_op jit(solution)/shard_map/all_to_all | solution.py:76
  27.6 45.2 %all_gather.7 = bf16[352,1024]{1,0:T(8,128)(2,1)} all-gather(bf16[88,1024]{1,0:T(8,128)(2,1)S(1)} %copy-done.108), channel_id=1, replica_groups=mesh['out'=2,'inn'=8,'narrow'=2] {'out','narrow'}, dimensions={0}, use_global_device_ids=true | all-gather | bytes 901120 | tf_op jit(solution)/shard_map/all_gather | solution.py:237
  84.4 3.9 collective-permute-done.24
  93.9 4.5 collective-permute-done.28
  103.7 3.7 fusion.556
  109.1 3.0 collective-permute-start.7
  128.6 4.4 fusion.472
  179.3 5.3 all-to-all-start.1
  188.0 2.8 all-to-all-done.1
  193.2 5.3 all-to-all-start.2
  209.7 3.8 gather_fusion.2
  214.1 4.6 collective-permute-done.10
  218.8 11.7 %collective-permute-done.12 = bf16[128,1024]{1,0:T(8,128)(2,1)} collective-permute-done((bf16[128,1024]{1,0:T(8,128)(2,1)}, bf16[128,1024]{1,0:T(8,128)(2,1)}, u32[]{:S(2)}, u32[]{:S(2)}) %collective-permute-start.12) | collective-permute-done | bytes 262176 | tf_op jit(solution)/shard_map/ppermute | solution.py:26
  230.5 8.6 %collective-permute-done.14 = bf16[128,1024]{1,0:T(8,128)(2,1)} collective-permute-done((bf16[128,1024]{1,0:T(8,128)(2,1)}, bf16[128,1024]{1,0:T(8,128)(2,1)}, u32[]{:S(2)}, u32[]{:S(2)}) %collective-permute-start.14) | collective-permute-done | bytes 262176 | tf_op jit(solution)/shard_map/ppermute | solution.py:26
  248.0 3.8 gather_fusion.1
  251.8 3.9 fusion.566
  257.3 4.4 convolution_convert_fusion.3
  271.0 5.2 collective-permute-done.36
  277.6 2.9 collective-permute-done.34
  283.3 4.2 collective-permute-done.22
  287.4 3.8 collective-permute-done.20
  296.2 4.0 all-to-all-start.3
  300.2 5.2 convolution_convert_fusion.4
  308.0 3.6 convolution_convert_fusion.6
  311.6 5.2 all-to-all-start.7
  316.9 3.1 multiply_reduce_fusion.8
  378.7 4.4 fusion.469
  411.1 4.4 bitcast_dynamic-update-slice_fusion.29
  423.7 3.0 fusion.24
  435.0 7.7 %all-to-all-start.6 = ((bf16[32,32,704]{2,1,0:T(8,128)(2,1)}), bf16[32,32,704]{2,1,0:T(8,128)(2,1)}, u32[]{:S(2)}, u32[]{:S(2)}) async-start(bf16[32,32,704]{2,1,0:T(8,128)(2,1)} %bitcast.786), calls=%async_computation.6 | async-start | bytes 3145728 | tf_op jit(solution)/shard_map/all_to_all | solution.py:76
  442.8 3.6 multiply_reduce_fusion.3
  449.8 30.7 %collective-permute-done.38 = f32[3,384]{1,0:T(4,128)S(1)} collective-permute-done((f32[3,384]{1,0:T(4,128)S(1)}, f32[3,384]{1,0:T(4,128)S(1)}, u32[]{:S(2)}, u32[]{:S(2)}) %collective-permute-start.38) | collective-permute-done | bytes 4640 | tf_op jit(solution)/shard_map/ppermute | solution.py:32
  481.6 2.9 convolution_convert_fusion.5
  484.5 2.8 all-to-all-start.4
  487.3 3.0 convolution_convert_fusion.1
  490.3 28.9 %all-to-all-done.4 = bf16[32,32,640]{2,1,0:T(8,128)(2,1)S(1)} async-done(((bf16[32,32,640]{2,1,0:T(8,128)(2,1)}), bf16[32,32,640]{2,1,0:T(8,128)(2,1)S(1)}, u32[]{:S(2)}, u32[]{:S(2)}) %all-to-all-start.4) | async-done | bytes 1310752 | tf_op jit(solution)/shard_map/all_to_all | solution.py:76
  520.3 3.8 all-to-all-start.5
  524.1 3.4 convolution_convert_fusion.2
  534.7 2.8 collective-permute-start.45
  538.4 28.4 %collective-permute-done.45 = bf16[128,1024]{1,0:T(8,128)(2,1)} collective-permute-done((bf16[128,1024]{1,0:T(8,128)(2,1)}, bf16[128,1024]{1,0:T(8,128)(2,1)}, u32[]{:S(2)}, u32[]{:S(2)}) %collective-permute-start.45) | collective-permute-done | bytes 262176 | tf_op jit(solution)/shard_map/ppermute | solution.py:26
  566.8 5.3 collective-permute-done.43
  573.6 3.8 collective-permute-start.46
  577.4 3.5 collective-permute-done.46
  587.1 3.9 collective-permute-done.49
  592.2 3.1 collective-permute-done.50
  597.9 2.6 convert_reduce_fusion.1
  600.5 3.2 reshape.963
  605.3 3.6 reshape.964
  (761 shorter events, 275.4 us)
Async XLA Ops:
  10.1 68.7 %collective-permute-start = (bf16[128,1024]{1,0:T(8,128)(2,1)}, bf16[128,1024]{1,0:T(8,128)(2,1)}, u32[]{:S(2)}, u32[]{:S(2)}) collective-permute-start(bf16[128,1024]{1,0:T(8,128)(2,1)} %fusion.36), channel_id=1, source_target_pairs={{0,2},{2,0},{4,6},{6,4},{8,10},{10,8},{12,14},{14,12},{1,3},{3,1},... | collective-permute-start | bytes 786440 | tf_op jit(solution)/shard_map/ppermute | solution.py:26
  10.5 70.8 %collective-permute-start.1 = (bf16[128,1024]{1,0:T(8,128)(2,1)}, bf16[128,1024]{1,0:T(8,128)(2,1)}, u32[]{:S(2)}, u32[]{:S(2)}) collective-permute-start(bf16[128,1024]{1,0:T(8,128)(2,1)} %fusion.36), channel_id=1, source_target_pairs={{0,4},{2,6},{4,0},{6,2},{8,12},{10,14},{12,8},{14,10},{1,5},{3,7},... | collective-permute-start | bytes 786440 | tf_op jit(solution)/shard_map/ppermute | solution.py:26
  13.0 77.7 %collective-permute-start.3 = (bf16[128,1024]{1,0:T(8,128)(2,1)}, bf16[128,1024]{1,0:T(8,128)(2,1)}, u32[]{:S(2)}, u32[]{:S(2)}) collective-permute-start(bf16[128,1024]{1,0:T(8,128)(2,1)} %fusion.36), channel_id=1, source_target_pairs={{0,8},{2,10},{4,12},{6,14},{8,0},{10,2},{12,4},{14,6},{1,9},{3,11}... | collective-permute-start | bytes 786440 | tf_op jit(solution)/shard_map/ppermute | solution.py:26
  14.6 76.7 %collective-permute-start.5 = (bf16[128,1024]{1,0:T(8,128)(2,1)}, bf16[128,1024]{1,0:T(8,128)(2,1)}, u32[]{:S(2)}, u32[]{:S(2)}) collective-permute-start(bf16[128,1024]{1,0:T(8,128)(2,1)} %fusion.36), channel_id=1, source_target_pairs={{0,12},{2,14},{4,8},{6,10},{8,4},{10,6},{12,0},{14,2},{1,13},{3,15... | collective-permute-start | bytes 786440 | tf_op jit(solution)/shard_map/ppermute | solution.py:26
  17.9 85.8 %all-to-all-start = ((bf16[32,32,640]{2,1,0:T(8,128)(2,1)}), bf16[32,32,640]{2,1,0:T(8,128)(2,1)}, u32[]{:S(2)}, u32[]{:S(2)}) async-start(bf16[32,32,640]{2,1,0:T(8,128)(2,1)} %bitcast.13), calls=%async_computation | async-start | bytes 2621440 | tf_op jit(solution)/shard_map/all_to_all | solution.py:76
  24.4 174.2 %all-gather.2.cloned.1.call-start = ((), (), s32[]{:S(2)}) async-start(), calls=%async_computation.8 | async-start | bytes 2162688 | tf_op jit(solution)/shard_map/all_gather | solution.py:238
  25.1 57.3 %collective-permute-start.23 = (bf16[128,1024]{1,0:T(8,128)(2,1)}, bf16[128,1024]{1,0:T(8,128)(2,1)}, u32[]{:S(2)}, u32[]{:S(2)}) collective-permute-start(bf16[128,1024]{1,0:T(8,128)(2,1)} %bitcast.81), channel_id=1, source_target_pairs={{0,2},{2,0},{4,6},{6,4},{8,10},{10,8},{12,14},{14,12},{1,3},{3,1},... | collective-permute-start | bytes 786440 | tf_op jit(solution)/shard_map/ppermute | solution.py:26
  78.8 9.6 %collective-permute-start.24 = (bf16[128,1024]{1,0:T(8,128)(2,1)}, bf16[128,1024]{1,0:T(8,128)(2,1)S(1)}, u32[]{:S(2)}, u32[]{:S(2)}) collective-permute-start(bf16[128,1024]{1,0:T(8,128)(2,1)} %bitcast.81), channel_id=1, source_target_pairs={{0,4},{2,6},{4,0},{6,2},{8,12},{10,14},{12,8},{14,10},{1,5},{3,7},... | collective-permute-start | bytes 786440 | tf_op jit(solution)/shard_map/ppermute | solution.py:26
  81.3 12.6 %collective-permute-start.26 = (bf16[128,1024]{1,0:T(8,128)(2,1)}, bf16[128,1024]{1,0:T(8,128)(2,1)}, u32[]{:S(2)}, u32[]{:S(2)}) collective-permute-start(bf16[128,1024]{1,0:T(8,128)(2,1)} %bitcast.81), channel_id=1, source_target_pairs={{0,8},{2,10},{4,12},{6,14},{8,0},{10,2},{12,4},{14,6},{1,9},{3,11}... | collective-permute-start | bytes 786440 | tf_op jit(solution)/shard_map/ppermute | solution.py:26
  82.4 16.0 %collective-permute-start.28 = (bf16[128,1024]{1,0:T(8,128)(2,1)}, bf16[128,1024]{1,0:T(8,128)(2,1)}, u32[]{:S(2)}, u32[]{:S(2)}) collective-permute-start(bf16[128,1024]{1,0:T(8,128)(2,1)} %bitcast.81), channel_id=1, source_target_pairs={{0,12},{2,14},{4,8},{6,10},{8,4},{10,6},{12,0},{14,2},{1,13},{3,15... | collective-permute-start | bytes 786440 | tf_op jit(solution)/shard_map/ppermute | solution.py:26
  88.4 10.0 %collective-permute-start.2 = (bf16[128,1024]{1,0:T(8,128)(2,1)}, bf16[128,1024]{1,0:T(8,128)(2,1)S(1)}, u32[]{:S(2)}, u32[]{:S(2)}) collective-permute-start(bf16[128,1024]{1,0:T(8,128)(2,1)} %collective-permute-done.1), channel_id=1, source_target_pairs={{0,2},{2,0},{4,6},{6,4},{8,10},{10,8},{12,14},{14,12},{1,3},{3,1},... | collective-permute-start | bytes 786440 | tf_op jit(solution)/shard_map/ppermute | solution.py:26
  90.8 12.2 %collective-permute-start.25 = (bf16[128,1024]{1,0:T(8,128)(2,1)S(1)}, bf16[128,1024]{1,0:T(8,128)(2,1)S(1)}, u32[]{:S(2)}, u32[]{:S(2)}) collective-permute-start(bf16[128,1024]{1,0:T(8,128)(2,1)S(1)} %collective-permute-done.24), channel_id=1, source_target_pairs={{0,2},{2,0},{4,6},{6,4},{8,10},{10,8},{12,14},{14,12},{1,3},{3,1},... | collective-permute-start | bytes 786440 | tf_op jit(solution)/shard_map/ppermute | solution.py:26
  91.3 8.6 %collective-permute-start.4 = (bf16[128,1024]{1,0:T(8,128)(2,1)}, bf16[128,1024]{1,0:T(8,128)(2,1)S(1)}, u32[]{:S(2)}, u32[]{:S(2)}) collective-permute-start(bf16[128,1024]{1,0:T(8,128)(2,1)} %collective-permute-done.3), channel_id=1, source_target_pairs={{0,2},{2,0},{4,6},{6,4},{8,10},{10,8},{12,14},{14,12},{1,3},{3,1},... | collective-permute-start | bytes 786440 | tf_op jit(solution)/shard_map/ppermute | solution.py:26
  93.9 7.0 %collective-permute-start.6 = (bf16[128,1024]{1,0:T(8,128)(2,1)}, bf16[128,1024]{1,0:T(8,128)(2,1)S(1)}, u32[]{:S(2)}, u32[]{:S(2)}) collective-permute-start(bf16[128,1024]{1,0:T(8,128)(2,1)} %collective-permute-done.5), channel_id=1, source_target_pairs={{0,2},{2,0},{4,6},{6,4},{8,10},{10,8},{12,14},{14,12},{1,3},{3,1},... | collective-permute-start | bytes 786440 | tf_op jit(solution)/shard_map/ppermute | solution.py:26
  98.4 88.0 %collective-permute-start.27 = (bf16[128,1024]{1,0:T(8,128)(2,1)}, bf16[128,1024]{1,0:T(8,128)(2,1)}, u32[]{:S(2)}, u32[]{:S(2)}) collective-permute-start(bf16[128,1024]{1,0:T(8,128)(2,1)} %collective-permute-done.26), channel_id=1, source_target_pairs={{0,2},{2,0},{4,6},{6,4},{8,10},{10,8},{12,14},{14,12},{1,3},{3,1},... | collective-permute-start | bytes 786440 | tf_op jit(solution)/shard_map/ppermute | solution.py:26
  98.4 109.7 %collective-permute-start.29 = (bf16[128,1024]{1,0:T(8,128)(2,1)}, bf16[128,1024]{1,0:T(8,128)(2,1)}, u32[]{:S(2)}, u32[]{:S(2)}) collective-permute-start(bf16[128,1024]{1,0:T(8,128)(2,1)} %collective-permute-done.28), channel_id=1, source_target_pairs={{0,2},{2,0},{4,6},{6,4},{8,10},{10,8},{12,14},{14,12},{1,3},{3,1},... | collective-permute-start | bytes 786440 | tf_op jit(solution)/shard_map/ppermute | solution.py:26
  109.1 13.0 %collective-permute-start.7 = (f32[3,384]{1,0:T(4,128)S(1)}, f32[3,384]{1,0:T(4,128)S(1)}, u32[]{:S(2)}, u32[]{:S(2)}) collective-permute-start(f32[3,384]{1,0:T(4,128)S(1)} %slice.322), channel_id=1, source_target_pairs={{0,16},{1,17},{2,18},{3,19},{4,20},{5,21},{6,22},{7,23},{8,24},{9,... | collective-permute-start | bytes 13832 | tf_op jit(solution)/shard_map/ppermute | solution.py:32
  179.3 11.5 %all-to-all-start.1 = ((bf16[8,128,128]{1,2,0:T(8,128)(2,1)}), bf16[8,128,128]{1,2,0:T(8,128)(2,1)}, u32[]{:S(2)}, u32[]{:S(2)}) async-start(bf16[8,128,128]{1,2,0:T(8,128)(2,1)} %copy.341), calls=%async_computation.1 | async-start | bytes 524288 | tf_op jit(solution)/shard_map/all_to_all | solution.py:293
  193.2 58.7 %all-to-all-start.2 = ((bf16[32,32,704]{2,1,0:T(8,128)(2,1)}), bf16[32,32,704]{2,1,0:T(8,128)(2,1)}, u32[]{:S(2)}, u32[]{:S(2)}) async-start(bf16[32,32,704]{2,1,0:T(8,128)(2,1)} %bitcast.787), calls=%async_computation.2 | async-start | bytes 3145728 | tf_op jit(solution)/shard_map/all_to_all | solution.py:76
  202.5 36.6 %collective-permute-start.9 = (bf16[128,1024]{1,0:T(8,128)(2,1)}, bf16[128,1024]{1,0:T(8,128)(2,1)}, u32[]{:S(2)}, u32[]{:S(2)}) collective-permute-start(bf16[128,1024]{1,0:T(8,128)(2,1)} %get-tuple-element.81), channel_id=1, source_target_pairs={{0,2},{2,0},{4,6},{6,4},{8,10},{10,8},{12,14},{14,12},{1,3},{3,1},... | collective-permute-start | bytes 786440 | tf_op jit(solution)/shard_map/ppermute | solution.py:26
  202.9 15.9 %collective-permute-start.10 = (bf16[128,1024]{1,0:T(8,128)(2,1)}, bf16[128,1024]{1,0:T(8,128)(2,1)}, u32[]{:S(2)}, u32[]{:S(2)}) collective-permute-start(bf16[128,1024]{1,0:T(8,128)(2,1)} %get-tuple-element.81), channel_id=1, source_target_pairs={{0,4},{2,6},{4,0},{6,2},{8,12},{10,14},{12,8},{14,10},{1,5},{3,7},... | collective-permute-start | bytes 786440 | tf_op jit(solution)/shard_map/ppermute | solution.py:26
  204.6 26.0 %collective-permute-start.12 = (bf16[128,1024]{1,0:T(8,128)(2,1)}, bf16[128,1024]{1,0:T(8,128)(2,1)}, u32[]{:S(2)}, u32[]{:S(2)}) collective-permute-start(bf16[128,1024]{1,0:T(8,128)(2,1)} %get-tuple-element.81), channel_id=1, source_target_pairs={{0,8},{2,10},{4,12},{6,14},{8,0},{10,2},{12,4},{14,6},{1,9},{3,11}... | collective-permute-start | bytes 786440 | tf_op jit(solution)/shard_map/ppermute | solution.py:26
  206.0 33.1 %collective-permute-start.14 = (bf16[128,1024]{1,0:T(8,128)(2,1)}, bf16[128,1024]{1,0:T(8,128)(2,1)}, u32[]{:S(2)}, u32[]{:S(2)}) collective-permute-start(bf16[128,1024]{1,0:T(8,128)(2,1)} %get-tuple-element.81), channel_id=1, source_target_pairs={{0,12},{2,14},{4,8},{6,10},{8,4},{10,6},{12,0},{14,2},{1,13},{3,15... | collective-permute-start | bytes 786440 | tf_op jit(solution)/shard_map/ppermute | solution.py:26
  218.8 23.7 %collective-permute-start.11 = (bf16[128,1024]{1,0:T(8,128)(2,1)}, bf16[128,1024]{1,0:T(8,128)(2,1)S(1)}, u32[]{:S(2)}, u32[]{:S(2)}) collective-permute-start(bf16[128,1024]{1,0:T(8,128)(2,1)} %collective-permute-done.10), channel_id=1, source_target_pairs={{0,2},{2,0},{4,6},{6,4},{8,10},{10,8},{12,14},{14,12},{1,3},{3,1},... | collective-permute-start | bytes 786440 | tf_op jit(solution)/shard_map/ppermute | solution.py:26
  230.5 14.3 %collective-permute-start.13 = (bf16[128,1024]{1,0:T(8,128)(2,1)}, bf16[128,1024]{1,0:T(8,128)(2,1)S(1)}, u32[]{:S(2)}, u32[]{:S(2)}) collective-permute-start(bf16[128,1024]{1,0:T(8,128)(2,1)} %collective-permute-done.12), channel_id=1, source_target_pairs={{0,2},{2,0},{4,6},{6,4},{8,10},{10,8},{12,14},{14,12},{1,3},{3,1},... | collective-permute-start | bytes 786440 | tf_op jit(solution)/shard_map/ppermute | solution.py:26
  239.1 8.1 %collective-permute-start.15 = (bf16[128,1024]{1,0:T(8,128)(2,1)}, bf16[128,1024]{1,0:T(8,128)(2,1)S(1)}, u32[]{:S(2)}, u32[]{:S(2)}) collective-permute-start(bf16[128,1024]{1,0:T(8,128)(2,1)} %collective-permute-done.14), channel_id=1, source_target_pairs={{0,2},{2,0},{4,6},{6,4},{8,10},{10,8},{12,14},{14,12},{1,3},{3,1},... | collective-permute-start | bytes 786440 | tf_op jit(solution)/shard_map/ppermute | solution.py:26
  262.9 6.9 %collective-permute-start.30 = (bf16[128,1024]{1,0:T(8,128)(2,1)S(1)}, bf16[128,1024]{1,0:T(8,128)(2,1)S(1)}, u32[]{:S(2)}, u32[]{:S(2)}) collective-permute-start(bf16[128,1024]{1,0:T(8,128)(2,1)S(1)} %get-tuple-element.124), channel_id=1, source_target_pairs={{0,2},{2,0},{4,6},{6,4},{8,10},{10,8},{12,14},{14,12},{1,3},{3,1},... | collective-permute-start | bytes 786440 | tf_op jit(solution)/shard_map/ppermute | solution.py:26
  265.4 17.8 %collective-permute-start.16 = (bf16[128,1024]{1,0:T(8,128)(2,1)S(1)}, bf16[128,1024]{1,0:T(8,128)(2,1)S(1)}, u32[]{:S(2)}, u32[]{:S(2)}) collective-permute-start(bf16[128,1024]{1,0:T(8,128)(2,1)S(1)} %get-tuple-element.131), channel_id=1, source_target_pairs={{0,2},{2,0},{4,6},{6,4},{8,10},{10,8},{12,14},{14,12},{1,3},{3,1},... | collective-permute-start | bytes 786440 | tf_op jit(solution)/shard_map/ppermute | solution.py:26
  266.1 10.1 %collective-permute-start.36 = (bf16[128,1024]{1,0:T(8,128)(2,1)S(1)}, bf16[128,1024]{1,0:T(8,128)(2,1)S(1)}, u32[]{:S(2)}, u32[]{:S(2)}) collective-permute-start(bf16[128,1024]{1,0:T(8,128)(2,1)S(1)} %get-tuple-element.129), channel_id=1, source_target_pairs={{0,12},{2,14},{4,8},{6,10},{8,4},{10,6},{12,0},{14,2},{1,13},{3,15... | collective-permute-start | bytes 786440 | tf_op jit(solution)/shard_map/ppermute | solution.py:26
  267.1 13.4 %collective-permute-start.34 = (bf16[128,1024]{1,0:T(8,128)(2,1)S(1)}, bf16[128,1024]{1,0:T(8,128)(2,1)S(1)}, u32[]{:S(2)}, u32[]{:S(2)}) collective-permute-start(bf16[128,1024]{1,0:T(8,128)(2,1)S(1)} %get-tuple-element.130), channel_id=1, source_target_pairs={{0,8},{2,10},{4,12},{6,14},{8,0},{10,2},{12,4},{14,6},{1,9},{3,11}... | collective-permute-start | bytes 786440 | tf_op jit(solution)/shard_map/ppermute | solution.py:26
  267.9 14.5 %collective-permute-start.32 = (bf16[128,1024]{1,0:T(8,128)(2,1)S(1)}, bf16[128,1024]{1,0:T(8,128)(2,1)S(1)}, u32[]{:S(2)}, u32[]{:S(2)}) collective-permute-start(bf16[128,1024]{1,0:T(8,128)(2,1)S(1)} %get-tuple-element.128), channel_id=1, source_target_pairs={{0,4},{2,6},{4,0},{6,2},{8,12},{10,14},{12,8},{14,10},{1,5},{3,7},... | collective-permute-start | bytes 786440 | tf_op jit(solution)/shard_map/ppermute | solution.py:26
  269.9 17.5 %collective-permute-start.22 = (bf16[128,1024]{1,0:T(8,128)(2,1)S(1)}, bf16[128,1024]{1,0:T(8,128)(2,1)S(1)}, u32[]{:S(2)}, u32[]{:S(2)}) collective-permute-start(bf16[128,1024]{1,0:T(8,128)(2,1)S(1)} %get-tuple-element.136), channel_id=1, source_target_pairs={{0,12},{2,14},{4,8},{6,10},{8,4},{10,6},{12,0},{14,2},{1,13},{3,15... | collective-permute-start | bytes 786440 | tf_op jit(solution)/shard_map/ppermute | solution.py:26
  276.2 15.1 %collective-permute-start.20 = (bf16[128,1024]{1,0:T(8,128)(2,1)S(1)}, bf16[128,1024]{1,0:T(8,128)(2,1)S(1)}, u32[]{:S(2)}, u32[]{:S(2)}) collective-permute-start(bf16[128,1024]{1,0:T(8,128)(2,1)S(1)} %get-tuple-element.137), channel_id=1, source_target_pairs={{0,8},{2,10},{4,12},{6,14},{8,0},{10,2},{12,4},{14,6},{1,9},{3,11}... | collective-permute-start | bytes 786440 | tf_op jit(solution)/shard_map/ppermute | solution.py:26
  280.5 12.0 %collective-permute-start.18 = (bf16[128,1024]{1,0:T(8,128)(2,1)S(1)}, bf16[128,1024]{1,0:T(8,128)(2,1)S(1)}, u32[]{:S(2)}, u32[]{:S(2)}) collective-permute-start(bf16[128,1024]{1,0:T(8,128)(2,1)S(1)} %get-tuple-element.135), channel_id=1, source_target_pairs={{0,4},{2,6},{4,0},{6,2},{8,12},{10,14},{12,8},{14,10},{1,5},{3,7},... | collective-permute-start | bytes 786440 | tf_op jit(solution)/shard_map/ppermute | solution.py:26
  296.2 15.5 %all-to-all-start.3 = ((bf16[128,8,128]{2,0,1:T(8,128)(2,1)}), bf16[128,8,128]{2,0,1:T(8,128)(2,1)}, u32[]{:S(2)}, u32[]{:S(2)}) async-start(bf16[128,8,128]{2,0,1:T(8,128)(2,1)} %bitcast.805), calls=%async_computation.3 | async-start | bytes 524288 | tf_op jit(solution)/shard_map/all_to_all | solution.py:313
  311.6 123.4 %all-to-all-start.7 = ((bf16[4,88,1024]{2,1,0:T(8,128)(2,1)}), bf16[4,88,1024]{2,1,0:T(8,128)(2,1)}, u32[]{:S(2)}, u32[]{:S(2)}) async-start(bf16[4,88,1024]{2,1,0:T(8,128)(2,1)} %bitcast.809), calls=%async_computation.7 | async-start | bytes 1441792 | tf_op jit(solution)/shard_map/all_to_all | solution.py:76
  383.0 28.1 %collective-permute-start.37 = (f32[2,128,128]{2,1,0:T(8,128)S(1)}, f32[2,128,128]{2,1,0:T(8,128)S(1)}, u32[]{:S(2)}, u32[]{:S(2)}) collective-permute-start(f32[2,128,128]{2,1,0:T(8,128)S(1)} %fusion.469), channel_id=1, source_target_pairs={{16,0},{17,1},{18,2},{19,3},{20,4},{21,5},{22,6},{23,7},{24,8},{25... | collective-permute-start | bytes 393224 | tf_op jit(solution)/shard_map/ppermute | solution.py:32
  435.0 49.5 %all-to-all-start.6 = ((bf16[32,32,704]{2,1,0:T(8,128)(2,1)}), bf16[32,32,704]{2,1,0:T(8,128)(2,1)}, u32[]{:S(2)}, u32[]{:S(2)}) async-start(bf16[32,32,704]{2,1,0:T(8,128)(2,1)} %bitcast.786), calls=%async_computation.6 | async-start | bytes 3145728 | tf_op jit(solution)/shard_map/all_to_all | solution.py:76
  447.1 33.3 %collective-permute-start.38 = (f32[3,384]{1,0:T(4,128)S(1)}, f32[3,384]{1,0:T(4,128)S(1)}, u32[]{:S(2)}, u32[]{:S(2)}) collective-permute-start(f32[3,384]{1,0:T(4,128)S(1)} %pad_add_fusion.3), channel_id=1, source_target_pairs={{16,0},{17,1},{18,2},{19,3},{20,4},{21,5},{22,6},{23,7},{24,8},{25... | collective-permute-start | bytes 13832 | tf_op jit(solution)/shard_map/ppermute | solution.py:32
  484.5 34.7 %all-to-all-start.4 = ((bf16[32,32,640]{2,1,0:T(8,128)(2,1)}), bf16[32,32,640]{2,1,0:T(8,128)(2,1)S(1)}, u32[]{:S(2)}, u32[]{:S(2)}) async-start(bf16[32,32,640]{2,1,0:T(8,128)(2,1)} %bitcast.803), calls=%async_computation.4 | async-start | bytes 2621440 | tf_op jit(solution)/shard_map/all_to_all | solution.py:76
  520.3 94.4 %all-to-all-start.5 = ((bf16[32,32,1024]{2,1,0:T(8,128)(2,1)}), bf16[32,32,1024]{2,1,0:T(8,128)(2,1)S(1)}, u32[]{:S(2)}, u32[]{:S(2)}) async-start(bf16[32,32,1024]{2,1,0:T(8,128)(2,1)} %bitcast.156), calls=%async_computation.5 | async-start | bytes 4194304 | tf_op jit(solution)/shard_map/all_to_all | solution.py:76
  531.5 6.9 %collective-permute-start.39 = (bf16[128,1024]{1,0:T(8,128)(2,1)S(1)}, bf16[128,1024]{1,0:T(8,128)(2,1)S(1)}, u32[]{:S(2)}, u32[]{:S(2)}) collective-permute-start(bf16[128,1024]{1,0:T(8,128)(2,1)S(1)} %get-tuple-element.117), channel_id=1, source_target_pairs={{0,2},{2,0},{4,6},{6,4},{8,10},{10,8},{12,14},{14,12},{1,3},{3,1},... | collective-permute-start | bytes 786440 | tf_op jit(solution)/shard_map/ppermute | solution.py:26
  534.7 32.0 %collective-permute-start.45 = (bf16[128,1024]{1,0:T(8,128)(2,1)}, bf16[128,1024]{1,0:T(8,128)(2,1)}, u32[]{:S(2)}, u32[]{:S(2)}) collective-permute-start(bf16[128,1024]{1,0:T(8,128)(2,1)} %get-tuple-element.122), channel_id=1, source_target_pairs={{0,12},{2,14},{4,8},{6,10},{8,4},{10,6},{12,0},{14,2},{1,13},{3,15... | collective-permute-start | bytes 786440 | tf_op jit(solution)/shard_map/ppermute | solution.py:26
  537.5 34.5 %collective-permute-start.43 = (bf16[128,1024]{1,0:T(8,128)(2,1)}, bf16[128,1024]{1,0:T(8,128)(2,1)}, u32[]{:S(2)}, u32[]{:S(2)}) collective-permute-start(bf16[128,1024]{1,0:T(8,128)(2,1)} %get-tuple-element.123), channel_id=1, source_target_pairs={{0,8},{2,10},{4,12},{6,14},{8,0},{10,2},{12,4},{14,6},{1,9},{3,11}... | collective-permute-start | bytes 786440 | tf_op jit(solution)/shard_map/ppermute | solution.py:26
  538.1 34.0 %collective-permute-start.41 = (bf16[128,1024]{1,0:T(8,128)(2,1)}, bf16[128,1024]{1,0:T(8,128)(2,1)}, u32[]{:S(2)}, u32[]{:S(2)}) collective-permute-start(bf16[128,1024]{1,0:T(8,128)(2,1)} %get-tuple-element.121), channel_id=1, source_target_pairs={{0,4},{2,6},{4,0},{6,2},{8,12},{10,14},{12,8},{14,10},{1,5},{3,7},... | collective-permute-start | bytes 786440 | tf_op jit(solution)/shard_map/ppermute | solution.py:26
  573.6 7.4 %collective-permute-start.46 = (f32[128,128]{1,0:T(8,128)S(1)}, f32[128,128]{1,0:T(8,128)S(1)}, u32[]{:S(2)}, u32[]{:S(2)}) collective-permute-start(f32[128,128]{1,0:T(8,128)S(1)} %pad_maximum_fusion.2), channel_id=1, source_target_pairs={{0,16},{16,0},{1,17},{17,1},{2,18},{18,2},{3,19},{19,3},{4,20},{20... | collective-permute-start | bytes 196616 | tf_op jit(solution)/shard_map/ppermute | solution.py:26
  582.3 4.3 collective-permute-start.48
  586.7 4.3 collective-permute-start.49
  (189 other events, 1281.0 us)
Sparse Core Ops, SparseCore 0:
  28.3 66.7 all-gather.1
